TPU v7x, 512 devices: a whole 4x4x16 slice. The times are simulated.
512 devices in a mesh: dp: 16 (over z_lo, y), fsdp: 32 (over z_hi, x, core).
Axes of the slice: x: 4, y: 4, z: 16 (z_hi: 4, z_lo: 4; z = z_hi * 4 + z_lo), core: 2. Of those that a mesh axis runs over, the one named last changes fastest.
Arguments:
- tokens: bfloat16 [131072, 8192], P(('dp', 'fsdp')), may hold values from -6 to 6
- grad_hidden: bfloat16 [131072, 256], P(('dp', 'fsdp')), may hold values from -0.06591797 to 0.06591797
- momentum: float32 [16, 8192, 256], P('dp', 'fsdp'), may hold values from -6 to 6
- kept: int32 [16], replicated, may hold values from 0 to 63, as said below
Outputs:
- new_momentum: float32 [16, 8192, 256], P('dp', 'fsdp')
- update: float32 [8192, 256], P('fsdp')
Inputs may be any that keep to these rules, and one draw needn't show every extreme that they name: `kept`: 16 different frequencies in increasing order, one fixed set used for every block; it contains 0 and 63.
All inputs are finite; a program needn't handle non-finite values.
Results may differ from a plain program's by a relative error of at most 0.019.
Values may be sent and summed in bfloat16 or wider, within the bound.
No kernel may reach another device: no remote copies, remote signals or barrier semaphores. Data moves between devices by JAX's collectives and lax.ppermute only.
A program may use at most 64 MiB of HBM per device.

v0:
```python
import math

import jax
import jax.numpy as jnp
from jax import lax
from jax.sharding import PartitionSpec as P

SPAN = 64
KEEP = 16


def kept_basis(kept):
    freq = kept.astype(jnp.float32)[:, None]
    place = jnp.arange(SPAN).astype(jnp.float32)[None, :]
    scale = jnp.where(kept == 0, math.sqrt(1.0 / SPAN), math.sqrt(2.0 / SPAN)).astype(jnp.float32)
    return scale[:, None] * jnp.cos(math.pi * (2.0 * place + 1.0) * freq / (2.0 * SPAN))


def on_device(tokens, grad_hidden, momentum, kept):
    rows = momentum.shape[1]
    cols = momentum.shape[2]
    grads = lax.psum_scatter(
        lax.dot_general(
            tokens, grad_hidden, (((0,), (0,)), ((), ())), preferred_element_type=jnp.float32
        ).astype(jnp.bfloat16),
        "fsdp",
        scatter_dimension=0,
        tiled=True,
    ).astype(jnp.float32)
    moment = 0.9 * momentum[0] + grads
    basis = kept_basis(kept)
    high = lax.Precision.HIGHEST
    blocks = moment.reshape(rows // SPAN, SPAN, cols // SPAN, SPAN)
    coeffs = jnp.einsum("kn,anbm,lm->abkl", basis, blocks, basis, precision=high)
    back = jnp.einsum("kn,abkl,lm->anbm", basis, coeffs, basis, precision=high)
    new_momentum = (blocks - back).reshape(1, rows, cols)
    count_blocks = rows // SPAN * (cols // SPAN)
    sent = coeffs.reshape(1, count_blocks, KEEP * KEEP).astype(jnp.bfloat16)
    every = lax.all_gather(sent, "dp", axis=0, tiled=True)
    total = jnp.sum(every.astype(jnp.float32), axis=0)
    mean = (total / lax.axis_size("dp")).reshape(rows // SPAN, cols // SPAN, KEEP, KEEP)
    update = 4.0 * jnp.einsum("kn,abkl,lm->anbm", basis, mean, basis, precision=high)
    return (new_momentum, update.reshape(rows, cols))


def solution(mesh):
    in_specs = (P(("dp", "fsdp"), None), P(("dp", "fsdp"), None), P("dp", "fsdp", None), P())
    out_specs = (P("dp", "fsdp", None), P("fsdp", None))
    return jax.shard_map(
        on_device, mesh=mesh, in_specs=in_specs, out_specs=out_specs, check_vma=False
    )
```

profile of v0, /device:TPU:6, one launch (start us, length us, event | category | flops | bytes accessed | tf_op | source)
XLA Modules:
  0.0 212.5 jit_solution(13641995962703867559)
XLA Ops:
  7.2 0.0 copy-start
  7.2 0.0 reduce-scatter.2.cloned.1.call-start
  7.2 0.8 copy-done
  8.1 5.4 %convolution_convert_fusion = bf16[8192,256]{1,0:T(8,128)(2,1)} fusion(bf16[256,8192]{1,0:T(8,128)(2,1)} %param.4, bf16[256,256]{1,0:T(8,128)(2,1)S(1)} %copy-done), kind=kOutput, calls=%fused_computation | convolution fusion | flops 1075838976 | bytes 8519680 | tf_op jit(solution)/shard_map/dot_general | solution.py:23
  13.5 0.0 copy-start.2
  13.5 0.0 copy-start.1
  13.5 0.0 reduce-scatter.2.cloned.1.call-update
  13.5 0.6 copy-done.2
  14.2 141.6 %reduce-scatter.2.cloned.1.call-done = bf16[256,256]{1,0:T(8,128)(2,1)} async-done(((bf16[8192,256]{1,0:T(8,128)(2,1)}), bf16[256,256]{1,0:T(8,128)(2,1)}) %reduce-scatter.2.cloned.1.call-update) | async-done | bytes 131088 | tf_op jit(solution)/shard_map/reduce_scatter | solution.py:22
  155.8 0.0 copy-done.1
  155.8 0.9 bitcast_add_fusion
  156.7 0.2 reshape.45
  156.9 0.4 fusion.2
  157.4 0.4 fusion.43
  157.8 0.4 fusion.8
  158.2 1.0 fusion.1
  159.3 0.3 copy.18
  159.6 1.0 reshape.46
  160.6 0.1 convert_element_type.38
  160.8 41.9 %all_gather.3 = bf16[16,16,256]{2,1,0:T(8,128)(2,1)S(1)} all-gather(bf16[1,16,256]{2,1,0:T(8,128)(2,1)S(1)} %convert_element_type.38), channel_id=1, replica_groups=mesh['dp'=16,'fsdp'=32] {'dp'}, dimensions={0}, use_global_device_ids=true | all-gather | bytes 139264 | tf_op jit(solution)/shard_map/all_gather | solution.py:39
  202.7 0.1 div.18
  202.8 0.4 fusion.5
  203.3 1.0 fusion
  204.3 0.3 copy.20
  204.7 1.0 reshape.47
  (5 shorter events, 0.0 us)
Async XLA Ops:
  7.2 0.9 copy-start
  7.2 148.6 %reduce-scatter.2.cloned.1.call-start = ((), (), s32[]{:S(2)}) async-start(), calls=%async_computation.1 | async-start | bytes 4325376 | tf_op jit(solution)/shard_map/reduce_scatter | solution.py:22
  13.5 0.7 copy-start.2
  13.5 142.2 %copy-start.1 = (f32[1,256,256]{2,1,0:T(8,128)S(1)}, f32[1,256,256]{2,1,0:T(8,128)}, u32[]{:S(2)}) copy-start(f32[1,256,256]{2,1,0:T(8,128)} %param.6) | copy-start | bytes 786436
Sparse Core Ops, SparseCore 0:
  13.7 142.0 reduce-scatter.1
where the time goes:
time: 213 us
  waiting for transfers between devices  142 us (67%)
  blocking collectives  41.9 us (20%)
  between operations  14.1 us (7%)
  matrix products  9.18 us (4%)
  local copies, waits for them, and re-layouts  4.71 us (2%)
    reduce_scatter x1, waiting for transfers between devices, on_device(): lax.psum_scatter(lax.dot_general(tokens, grad_hidden, (((0,), (0,)), ((),...  142 us
    all_gather x1, blocking collectives, on_device(): every = lax.all_gather(sent, 'dp', axis=0, tiled=True)  41.9 us
    dot_general x1, matrix products, on_device(): lax.dot_general(tokens, grad_hidden, (((0,), (0,)), ((), ())), preferred_...  5.43 us
  transfers between devices with their start and end apart: 1, of which 1 were waited for; matrix products, arithmetic and copies ran while one was open for 0% of the time, Pallas kernels for 0%

commit v1 on v0

v1 whole, which is shorter than its diff:
```python
import functools
import math

import jax
import jax.numpy as jnp
from jax import lax
from jax.experimental import pallas as pl
from jax.experimental.pallas import tpu as pltpu
from jax.sharding import PartitionSpec as P

SPAN = 64
KEEP = 16
UNIT = 256
RING = 4
HIGH = lax.Precision.HIGHEST
BF16 = jnp.bfloat16
F32 = jnp.float32

MASKS = ((0, 3, 1, 2), (0, 1, 3, 2))


def pairs(step):
    out = []
    for zh in range(RING):
        for x in range(RING):
            for c in range(2):
                a, b, d = step(zh, x, c)
                out.append(((zh * RING + x) * 2 + c, (a * RING + b) * 2 + d))
    return out


CORE = pairs(lambda zh, x, c: (zh, x, 1 - c))
X1 = pairs(lambda zh, x, c: (zh, x ^ MASKS[c][2], c))
X2 = pairs(lambda zh, x, c: (zh, x ^ MASKS[c][1], c))
Z1 = pairs(lambda zh, x, c: (zh ^ MASKS[c][2], x, c))
Z2 = pairs(lambda zh, x, c: (zh ^ MASKS[c][1], x, c))


def product_kernel(flip, places, me_ref, tokens_ref, hidden_ref, out_ref, held, sems):
    me = me_ref[0]
    c = me % 2
    x = (me // 2) % RING
    zh = me // (2 * RING)
    if flip:
        c = 1 - c
    copies = []
    for u, (p, q) in enumerate(places):
        mx = jnp.where(c == 0, MASKS[0][p], MASKS[1][p])
        mz = jnp.where(c == 0, MASKS[0][q], MASKS[1][q])
        block = ((zh ^ mz) * RING + (x ^ mx)) * 2 + c
        start = pl.multiple_of(block * UNIT, UNIT)
        copy = pltpu.make_async_copy(tokens_ref.at[:, pl.ds(start, UNIT)], held.at[u], sems.at[u])
        copy.start()
        copies.append(copy)
    left = hidden_ref[...].T
    for u, copy in enumerate(copies):
        copy.wait()
        out_ref[u] = jnp.dot(left, held[u], preferred_element_type=F32).astype(BF16)


def product(flip, places, me, tokens, hidden):
    n = len(places)
    toks = tokens.shape[0]
    cols = hidden.shape[1]
    return pl.pallas_call(
        functools.partial(product_kernel, flip, places),
        out_shape=jax.ShapeDtypeStruct((n, cols, UNIT), BF16),
        in_specs=[
            pl.BlockSpec(memory_space=pltpu.SMEM),
            pl.BlockSpec(memory_space=pl.ANY),
            pl.BlockSpec(memory_space=pltpu.VMEM),
        ],
        out_specs=pl.BlockSpec(memory_space=pltpu.VMEM),
        scratch_shapes=[pltpu.VMEM((n, toks, UNIT), BF16), pltpu.SemaphoreType.DMA((n,))],
        cost_estimate=pl.CostEstimate(
            flops=2 * n * toks * cols * UNIT, bytes_accessed=2 * n * UNIT * (toks + cols), transcendentals=0
        ),
    )(me, tokens, hidden)


def kept_basis(kept):
    freq = kept.astype(F32)[:, None]
    place = jnp.arange(SPAN).astype(F32)[None, :]
    scale = jnp.where(kept == 0, math.sqrt(1.0 / SPAN), math.sqrt(2.0 / SPAN)).astype(F32)
    return scale[:, None] * jnp.cos(math.pi * (2.0 * place + 1.0) * freq / (2.0 * SPAN))


def dot(a, b):
    return jnp.dot(a, b, precision=HIGH, preferred_element_type=F32)


def moment_kernel(part_ref, r1_ref, r2_ref, momentum_ref, wide_ref, tall_ref, out_ref, sent_ref):
    grad = part_ref[...].astype(F32) + r1_ref[...].astype(F32) + r2_ref[...].astype(F32)
    moment = 0.9 * momentum_ref[...] + grad.T
    wide = wide_ref[...]
    tall = tall_ref[...]
    coeffs = dot(dot(wide, moment), tall)
    half = coeffs.shape[0] // 2
    sent = jnp.concatenate([coeffs[:half], coeffs[half:]], axis=1).astype(BF16)
    for r in range(sent_ref.shape[0]):
        sent_ref[r] = sent
    out_ref[...] = moment - dot(tall, dot(coeffs, wide))


def update_kernel(every_ref, wide_ref, tall_ref, out_ref):
    total = jnp.sum(every_ref[...].astype(F32), axis=0)
    n = total.shape[1] // 2
    mean = jnp.concatenate([total[:, :n], total[:, n:]], axis=0) * (4.0 / every_ref.shape[0])
    out_ref[...] = dot(tall_ref[...], dot(mean, wide_ref[...]))


def on_device(tokens, grad_hidden, momentum, kept):
    rows = momentum.shape[1]
    cols = momentum.shape[2]
    n_dp = lax.axis_size("dp")
    me = lax.axis_index("fsdp").astype(jnp.int32).reshape(1)
    early = [(p, q) for p in range(RING) for q in (2, 3)]
    late = [(p, q) for p in range(RING) for q in (0, 1)]

    def swap(a, perm):
        return lax.ppermute(a, "fsdp", perm)

    def add(a, b):
        return (a.astype(F32) + b.astype(F32)).astype(BF16)

    other_a = product(True, early, me, tokens, grad_hidden)
    got_a = swap(other_a, CORE)
    other_b = product(True, late, me, tokens, grad_hidden)
    got_b = swap(other_b, CORE)
    own_a = product(False, early, me, tokens, grad_hidden)
    own_b = product(False, late, me, tokens, grad_hidden)

    def along_x(own, got):
        away = add(own[4:8], got[4:8])
        back = swap(away, X1)
        near = add(own[2:4].astype(F32) + got[2:4].astype(F32), back[2:4])
        last = swap(near, X2)
        return add(own[0:2].astype(F32) + got[0:2].astype(F32) + back[0:2].astype(F32), last)

    a = along_x(own_a, got_a)
    b = along_x(own_b, got_b)
    r3 = swap(a[1], Z1)
    r2 = swap(a[0], Z1)
    r1 = swap(add(b[1], r3), Z2)

    basis = kept_basis(kept)
    wide = jnp.kron(jnp.eye(cols // SPAN, dtype=F32), basis)
    tall = wide.T
    kw = wide.shape[0]
    new_momentum, sent = pl.pallas_call(
        moment_kernel,
        out_shape=(
            jax.ShapeDtypeStruct((rows, cols), F32),
            jax.ShapeDtypeStruct((n_dp, kw // 2, kw * 2), BF16),
        ),
    )(b[0], r2, r1, momentum[0], wide, tall)
    every = lax.all_to_all(sent, "dp", 0, 0, tiled=True)
    update = pl.pallas_call(update_kernel, out_shape=jax.ShapeDtypeStruct((rows, cols), F32))(every, wide, tall)
    return (new_momentum[None], update)


def solution(mesh):
    in_specs = (P(("dp", "fsdp"), None), P(("dp", "fsdp"), None), P("dp", "fsdp", None), P())
    out_specs = (P("dp", "fsdp", None), P("fsdp", None))
    return jax.shard_map(
        on_device, mesh=mesh, in_specs=in_specs, out_specs=out_specs, check_vma=False
    )
```

time: 213 us -> 105 us (0.49)
  waiting for transfers between devices: 142 us -> 11.1 us
  starting transfers between devices: 0.04 us -> 38 us
  Pallas kernels: 0 us -> 24.1 us
  blocking collectives: 41.9 us -> 18.6 us
  between operations: 14.1 us -> 0.88 us
  matrix products: 9.18 us -> 0 us
  other arithmetic: 0.97 us -> 8.76 us
  local copies, waits for them, and re-layouts: 4.71 us -> 2.23 us
    reduce_scatter x1 -> x0, waiting for transfers between devices: 142 us -> none  [on_device(): lax.psum_scatter(lax.dot_general(tokens, grad_hidden, (((0,), (0,)), ((),...]
    all_gather x1 -> x0, blocking collectives: 41.9 us -> none  [on_device(): every = lax.all_gather(sent, 'dp', axis=0, tiled=True)]
    ppermute x0 -> x9, starting transfers between devices: none -> 38 us  [swap(): return lax.ppermute(a, 'fsdp', perm)]
    pallas_call x0 -> x6, Pallas kernels: none -> 24.1 us  [the longest x4 18.6 us: product(): pl.pallas_call(functools.partial(product_kernel, flip, places), out_shape...]
    all_to_all x0 -> x1, blocking collectives: none -> 18.6 us  [on_device(): every = lax.all_to_all(sent, 'dp', 0, 0, tiled=True)]
    ppermute x0 -> x9, waiting for transfers between devices: none -> 11.1 us  [swap(): return lax.ppermute(a, 'fsdp', perm)]
    dot_general x7 -> x0, matrix products: 9.18 us -> none  [the longest x1 5.43 us: on_device(): lax.dot_general(tokens, grad_hidden, (((0,), (0,)), ((), ())), preferred_...]
    convert_element_type x1 -> x9, other arithmetic: 0.01 us -> 8.54 us  [the longest x7 8.53 us: add(): return (a.astype(F32) + b.astype(F32)).astype(BF16)]
  transfers between devices with their start and end apart: 1 -> 9, of which waited for: 1 -> 3; matrix products, arithmetic and copies ran while one was open for 0% -> 10% of each run, Pallas kernels for 0% -> 13%
where the time goes in v1:
time: 105 us; the launch traced here: 104 us
  starting transfers between devices  38 us (36%)
  Pallas kernels  24.1 us (23%)
  blocking collectives  18.6 us (18%)
  waiting for transfers between devices  11.1 us (11%)
  other arithmetic  8.76 us (8%)
  local copies, waits for them, and re-layouts  2.23 us (2%)
    ppermute x9, starting transfers between devices, swap(): return lax.ppermute(a, 'fsdp', perm)  38 us
    pallas_call x4, Pallas kernels, product(): pl.pallas_call(functools.partial(product_kernel, flip, places), out_shape...  18.6 us
    all_to_all x1, blocking collectives, on_device(): every = lax.all_to_all(sent, 'dp', 0, 0, tiled=True)  18.6 us
    ppermute x9, waiting for transfers between devices, swap(): return lax.ppermute(a, 'fsdp', perm)  11.1 us
    convert_element_type x7, other arithmetic, add(): return (a.astype(F32) + b.astype(F32)).astype(BF16)  8.53 us
    pallas_call x1, Pallas kernels, on_device(): pl.pallas_call(moment_kernel, out_shape=(jax.ShapeDtypeStruct((rows, cols...  3.09 us
    pallas_call x1, Pallas kernels, on_device(): pl.pallas_call(update_kernel, out_shape=jax.ShapeDtypeStruct((rows, cols)...  2.4 us
  transfers between devices with their start and end apart: 9, of which 3 were waited for; matrix products, arithmetic and copies ran while one was open for 10% of the time, Pallas kernels for 13%

profile of v1, /device:TPU:6, one launch (start us, length us, event | category | flops | bytes accessed | tf_op | source)
XLA Modules:
  0.0 103.6 jit_solution(17192241786378474122)
XLA Ops:
  0.6 0.0 copy-start.6
  0.6 4.6 %shard_map.62 = bf16[8,256,256]{2,1,0:T(8,128)(2,1)} custom-call(s32[1]{0:T(128)} %bitcast.me_ref, bf16[256,8192]{1,0:T(8,128)(2,1)} %tokens_ref.7, bf16[256,256]{1,0:T(8,128)(2,1)} %hidden_ref.7), custom_call_target="tpu_custom_call" | custom-call | flops 268435456 | bytes 2097152 | tf_op jit(solution)/shard_map/pallas_call | solution.py:65
  5.3 1.9 %collective-permute-start.3 = (bf16[8,256,256]{2,1,0:T(8,128)(2,1)}, bf16[8,256,256]{2,1,0:T(8,128)(2,1)}, u32[]{:S(2)}, u32[]{:S(2)}) collective-permute-start(bf16[8,256,256]{2,1,0:T(8,128)(2,1)} %shard_map.62), channel_id=1, source_target_pairs={{0,1},{1,0},{2,3},{3,2},{4,5},{5,4},{6,7},{7,6},{8,9},{9,8},{10,11... | collective-permute-start | bytes 3145736 | tf_op jit(solution)/shard_map/ppermute | solution.py:121
  7.2 4.6 %shard_map.60 = bf16[8,256,256]{2,1,0:T(8,128)(2,1)} custom-call(s32[1]{0:T(128)} %bitcast.me_ref, bf16[256,8192]{1,0:T(8,128)(2,1)} %tokens_ref.7, bf16[256,256]{1,0:T(8,128)(2,1)} %hidden_ref.7), custom_call_target="tpu_custom_call" | custom-call | flops 268435456 | bytes 2097152 | tf_op jit(solution)/shard_map/pallas_call | solution.py:65
  11.8 2.4 %collective-permute-start = (bf16[8,256,256]{2,1,0:T(8,128)(2,1)}, bf16[8,256,256]{2,1,0:T(8,128)(2,1)S(1)}, u32[]{:S(2)}, u32[]{:S(2)}) collective-permute-start(bf16[8,256,256]{2,1,0:T(8,128)(2,1)} %shard_map.60), channel_id=1, source_target_pairs={{0,1},{1,0},{2,3},{3,2},{4,5},{5,4},{6,7},{7,6},{8,9},{9,8},{10,11... | collective-permute-start | bytes 3145736 | tf_op jit(solution)/shard_map/ppermute | solution.py:121
  14.2 0.0 copy-done.6
  14.3 4.6 %shard_map.61 = bf16[8,256,256]{2,1,0:T(8,128)(2,1)} custom-call(s32[1]{0:T(128)} %bitcast.me_ref, bf16[256,8192]{1,0:T(8,128)(2,1)} %tokens_ref.7, bf16[256,256]{1,0:T(8,128)(2,1)} %hidden_ref.7), custom_call_target="tpu_custom_call" | custom-call | flops 268435456 | bytes 2097152 | tf_op jit(solution)/shard_map/pallas_call | solution.py:65
  18.9 0.0 copy-start.1
  18.9 4.7 %shard_map.59 = bf16[8,256,256]{2,1,0:T(8,128)(2,1)} custom-call(s32[1]{0:T(128)} %bitcast.me_ref, bf16[256,8192]{1,0:T(8,128)(2,1)} %tokens_ref.7, bf16[256,256]{1,0:T(8,128)(2,1)} %hidden_ref.7), custom_call_target="tpu_custom_call" | custom-call | flops 268435456 | bytes 2097152 | tf_op jit(solution)/shard_map/pallas_call | solution.py:65
  23.6 0.0 copy-start
  23.6 0.0 collective-permute-done.3
  23.7 0.0 copy-done.1
  23.7 1.2 %add_convert_fusion = bf16[4,256,256]{2,1,0:T(8,128)(2,1)S(1)} fusion(bf16[8,256,256]{2,1,0:T(8,128)(2,1)} %collective-permute-done.3, bf16[8,256,256]{2,1,0:T(8,128)(2,1)S(1)} %copy-done.1), kind=kLoop, calls=%fused_computation | loop fusion | flops 1048576 | bytes 1572864 | tf_op jit(solution)/shard_map/convert_element_type | solution.py:124
  24.9 2.7 %collective-permute-start.4 = (bf16[4,256,256]{2,1,0:T(8,128)(2,1)S(1)}, bf16[4,256,256]{2,1,0:T(8,128)(2,1)S(1)}, u32[]{:S(2)}, u32[]{:S(2)}) collective-permute-start(bf16[4,256,256]{2,1,0:T(8,128)(2,1)S(1)} %add_convert_fusion), channel_id=1, source_target_pairs={{0,2},{1,7},{2,0},{3,5},{4,6},{5,3},{6,4},{7,1},{8,10},{9,15},{10,... | collective-permute-start | bytes 1572872 | tf_op jit(solution)/shard_map/ppermute | solution.py:121
  27.7 0.1 cosine_multiply_fusion
  27.8 0.0 collective-permute-done
  27.8 2.0 %add_convert_fusion.1 = bf16[4,256,256]{2,1,0:T(8,128)(2,1)} fusion(bf16[8,256,256]{2,1,0:T(8,128)(2,1)S(1)} %collective-permute-done, bf16[8,256,256]{2,1,0:T(8,128)(2,1)} %shard_map.59), kind=kLoop, calls=%fused_computation.1 | loop fusion | flops 1048576 | bytes 1572864 | tf_op jit(solution)/shard_map/convert_element_type | solution.py:124
  29.7 3.1 %collective-permute-start.1 = (bf16[4,256,256]{2,1,0:T(8,128)(2,1)}, bf16[4,256,256]{2,1,0:T(8,128)(2,1)}, u32[]{:S(2)}, u32[]{:S(2)}) collective-permute-start(bf16[4,256,256]{2,1,0:T(8,128)(2,1)} %add_convert_fusion.1), channel_id=1, source_target_pairs={{0,2},{1,7},{2,0},{3,5},{4,6},{5,3},{6,4},{7,1},{8,10},{9,15},{10,... | collective-permute-start | bytes 1572872 | tf_op jit(solution)/shard_map/ppermute | solution.py:121
  32.9 3.1 %collective-permute-done.4 = bf16[4,256,256]{2,1,0:T(8,128)(2,1)S(1)} collective-permute-done((bf16[4,256,256]{2,1,0:T(8,128)(2,1)S(1)}, bf16[4,256,256]{2,1,0:T(8,128)(2,1)S(1)}, u32[]{:S(2)}, u32[]{:S(2)}) %collective-permute-start.4) | collective-permute-done | bytes 524320 | tf_op jit(solution)/shard_map/ppermute | solution.py:121
  36.0 0.0 copy-start.3
  36.0 1.9 %add_convert_fusion.3 = bf16[2,256,256]{2,1,0:T(8,128)(2,1)} fusion(bf16[4,256,256]{2,1,0:T(8,128)(2,1)S(1)} %collective-permute-done.4, bf16[8,256,256]{2,1,0:T(8,128)(2,1)} %collective-permute-done.3, bf16[8,256,256]{2,1,0:T(8,128)(2,1)S(1)} %copy-done.1), kind=kLoop, calls=%fused_computation.3 | loop fusion | flops 786432 | bytes 1048576 | tf_op jit(solution)/shard_map/convert_element_type | solution.py:124
  37.9 7.7 %collective-permute-start.5 = (bf16[2,256,256]{2,1,0:T(8,128)(2,1)}, bf16[2,256,256]{2,1,0:T(8,128)(2,1)}, u32[]{:S(2)}, u32[]{:S(2)}) collective-permute-start(bf16[2,256,256]{2,1,0:T(8,128)(2,1)} %add_convert_fusion.3), channel_id=1, source_target_pairs={{0,6},{1,3},{2,4},{3,1},{4,2},{5,7},{6,0},{7,5},{8,14},{9,11},{10,... | collective-permute-start | bytes 786440 | tf_op jit(solution)/shard_map/ppermute | solution.py:121
  45.7 0.0 copy-done.3
  45.7 0.1 broadcast_multiply_fusion
  45.8 0.1 mul.87.wide_ref
  45.9 0.0 copy-start.2
  45.9 0.7 copy.8
  46.6 0.0 collective-permute-done.1
  46.6 0.0 copy-done
  46.6 1.0 %add_convert_fusion.5 = bf16[2,256,256]{2,1,0:T(8,128)(2,1)S(1)} fusion(bf16[4,256,256]{2,1,0:T(8,128)(2,1)} %collective-permute-done.1, bf16[8,256,256]{2,1,0:T(8,128)(2,1)S(1)} %collective-permute-done, bf16[8,256,256]{2,1,0:T(8,128)(2,1)S(1)} %copy-done), kind=kLoop, calls=%fused_computation.5 | loop fusion | flops 786432 | bytes 1048576 | tf_op jit(solution)/shard_map/convert_element_type | solution.py:124
  47.7 2.8 %collective-permute-start.2 = (bf16[2,256,256]{2,1,0:T(8,128)(2,1)S(1)}, bf16[2,256,256]{2,1,0:T(8,128)(2,1)S(1)}, u32[]{:S(2)}, u32[]{:S(2)}) collective-permute-start(bf16[2,256,256]{2,1,0:T(8,128)(2,1)S(1)} %add_convert_fusion.5), channel_id=1, source_target_pairs={{0,6},{1,3},{2,4},{3,1},{4,2},{5,7},{6,0},{7,5},{8,14},{9,11},{10,... | collective-permute-start | bytes 786440 | tf_op jit(solution)/shard_map/ppermute | solution.py:121
  50.5 0.0 collective-permute-done.5
  50.5 1.2 %add_convert_fusion.2 = bf16[2,256,256]{2,1,0:T(8,128)(2,1)S(1)} fusion(bf16[2,256,256]{2,1,0:T(8,128)(2,1)} %collective-permute-done.5, bf16[4,256,256]{2,1,0:T(8,128)(2,1)} %copy-done.3, bf16[8,256,256]{2,1,0:T(8,128)(2,1)} %collective-permute-done.3, bf16[8,256,256]{2,1,0:T(8,128)(2,1)S(1)} %copy-done.1), kind=kLoop, calls=%fused_computation.2 | loop fusion | flops 1048576 | bytes 1310720 | tf_op jit(solution)/shard_map/convert_element_type | solution.py:124
  51.8 6.2 %collective-permute-start.7 = (bf16[256,256]{1,0:T(8,128)(2,1)S(1)}, bf16[256,256]{1,0:T(8,128)(2,1)S(1)}, u32[]{:S(2)}, u32[]{:S(2)}) collective-permute-start(bf16[256,256]{1,0:T(8,128)(2,1)S(1)} %get-tuple-element.6), channel_id=1, source_target_pairs={{0,8},{1,25},{2,10},{3,27},{4,12},{5,29},{6,14},{7,31},{8,0},{9,17... | collective-permute-start | bytes 393224 | tf_op jit(solution)/shard_map/ppermute | solution.py:121
  58.1 3.5 %collective-permute-start.6 = (bf16[256,256]{1,0:T(8,128)(2,1)S(1)}, bf16[256,256]{1,0:T(8,128)(2,1)S(1)}, u32[]{:S(2)}, u32[]{:S(2)}) collective-permute-start(bf16[256,256]{1,0:T(8,128)(2,1)S(1)} %get-tuple-element.7), channel_id=1, source_target_pairs={{0,8},{1,25},{2,10},{3,27},{4,12},{5,29},{6,14},{7,31},{8,0},{9,17... | collective-permute-start | bytes 393224 | tf_op jit(solution)/shard_map/ppermute | solution.py:121
  61.6 0.0 collective-permute-done.2
  61.6 1.1 %add_convert_fusion.4 = bf16[2,256,256]{2,1,0:T(8,128)(2,1)S(1)} fusion(bf16[2,256,256]{2,1,0:T(8,128)(2,1)S(1)} %collective-permute-done.2, bf16[4,256,256]{2,1,0:T(8,128)(2,1)} %collective-permute-done.1, bf16[8,256,256]{2,1,0:T(8,128)(2,1)S(1)} %collective-permute-done, bf16[8,256,256]{2,1,0:T(8,128)(2,1)S(1)} %copy-done), kind=kLoop, calls=%fused_computation.4 | loop fusion | flops 1048576 | bytes 1310720 | tf_op jit(solution)/shard_map/convert_element_type | solution.py:124
  62.7 2.6 %collective-permute-done.7 = bf16[256,256]{1,0:T(8,128)(2,1)S(1)} collective-permute-done((bf16[256,256]{1,0:T(8,128)(2,1)S(1)}, bf16[256,256]{1,0:T(8,128)(2,1)S(1)}, u32[]{:S(2)}, u32[]{:S(2)}) %collective-permute-start.7) | collective-permute-done | bytes 131104 | tf_op jit(solution)/shard_map/ppermute | solution.py:121
  65.3 7.5 %collective-permute-start.8 = (bf16[256,256]{1,0:T(8,128)(2,1)S(1)}, bf16[256,256]{1,0:T(8,128)(2,1)S(1)}, u32[]{:S(2)}, u32[]{:S(2)}) collective-permute-start(bf16[256,256]{1,0:T(8,128)(2,1)S(1)} %fusion), channel_id=1, source_target_pairs={{0,24},{1,9},{2,26},{3,11},{4,28},{5,13},{6,30},{7,15},{8,16},{9,1... | collective-permute-start | bytes 393224 | tf_op jit(solution)/shard_map/ppermute | solution.py:121
  72.8 0.7 slice_bitcast_fusion.3.part_ref
  73.5 0.0 collective-permute-done.6.r1_ref
  73.5 0.0 copy-start.4
  73.5 5.4 %collective-permute-done.8.r2_ref = bf16[256,256]{1,0:T(8,128)(2,1)S(1)} collective-permute-done((bf16[256,256]{1,0:T(8,128)(2,1)S(1)}, bf16[256,256]{1,0:T(8,128)(2,1)S(1)}, u32[]{:S(2)}, u32[]{:S(2)}) %collective-permute-start.8) | collective-permute-done | bytes 131104 | tf_op jit(solution)/shard_map/ppermute | solution.py:121
  78.9 0.0 copy-start.5
  78.9 0.0 copy-done.2
  78.9 0.0 copy-done.4
  78.9 0.6 copy-done.5
  79.5 3.1 %shard_map.63 = (f32[256,256]{1,0:T(8,128)}, bf16[16,32,128]{2,1,0:T(8,128)(2,1)}) custom-call(bf16[256,256]{1,0:T(8,128)(2,1)} %slice_bitcast_fusion.3.part_ref, bf16[256,256]{1,0:T(8,128)(2,1)} %copy-done.4, bf16[256,256]{1,0:T(8,128)(2,1)} %copy-done.5, f32[256,256]{1,0:T(8,128)} %bitcast.17, f32[64,256]{1,0:T(8,128)} %copy-done.2, f32[256,64]{1,0:T(8,128)} %bitcast.15), custom_call_target="tpu_custom_call" | custom-call | tf_op jit(solution)/shard_map/pallas_call | solution.py:150
  82.6 18.6 %all_to_all.5.every_ref = bf16[16,32,128]{2,1,0:T(8,128)(2,1)} all-to-all(bf16[16,32,128]{2,1,0:T(8,128)(2,1)} %get-tuple-element.5), channel_id=1, replica_groups=mesh['dp'=16,'fsdp'=32] {'dp'}, dimensions={0} | all-to-all | bytes 262144 | tf_op jit(solution)/shard_map/all_to_all | solution.py:157
  101.2 2.4 %shard_map.64 = f32[256,256]{1,0:T(8,128)} custom-call(bf16[16,32,128]{2,1,0:T(8,128)(2,1)} %all_to_all.5.every_ref, f32[64,256]{1,0:T(8,128)} %copy-done.2, f32[256,64]{1,0:T(8,128)} %bitcast.16), custom_call_target="tpu_custom_call" | custom-call | tf_op jit(solution)/shard_map/pallas_call | solution.py:158
  (6 shorter events, 0.1 us)
Async XLA Ops:
  0.6 13.6 %copy-start.6 = (s32[16]{0:T(128)S(1)}, s32[16]{0:T(128)}, u32[]{:S(2)}) copy-start(s32[16]{0:T(128)} %param.7) | copy-start | bytes 196
  5.3 18.4 %collective-permute-start.3 = (bf16[8,256,256]{2,1,0:T(8,128)(2,1)}, bf16[8,256,256]{2,1,0:T(8,128)(2,1)}, u32[]{:S(2)}, u32[]{:S(2)}) collective-permute-start(bf16[8,256,256]{2,1,0:T(8,128)(2,1)} %shard_map.62), channel_id=1, source_target_pairs={{0,1},{1,0},{2,3},{3,2},{4,5},{5,4},{6,7},{7,6},{8,9},{9,8},{10,11... | collective-permute-start | bytes 3145736 | tf_op jit(solution)/shard_map/ppermute | solution.py:121
  11.8 16.0 %collective-permute-start = (bf16[8,256,256]{2,1,0:T(8,128)(2,1)}, bf16[8,256,256]{2,1,0:T(8,128)(2,1)S(1)}, u32[]{:S(2)}, u32[]{:S(2)}) collective-permute-start(bf16[8,256,256]{2,1,0:T(8,128)(2,1)} %shard_map.60), channel_id=1, source_target_pairs={{0,1},{1,0},{2,3},{3,2},{4,5},{5,4},{6,7},{7,6},{8,9},{9,8},{10,11... | collective-permute-start | bytes 3145736 | tf_op jit(solution)/shard_map/ppermute | solution.py:121
  18.9 4.8 %copy-start.1 = (bf16[8,256,256]{2,1,0:T(8,128)(2,1)S(1)}, bf16[8,256,256]{2,1,0:T(8,128)(2,1)}, u32[]{:S(2)}) copy-start(bf16[8,256,256]{2,1,0:T(8,128)(2,1)} %shard_map.61) | copy-start | bytes 3145732
  23.6 23.0 %copy-start = (bf16[8,256,256]{2,1,0:T(8,128)(2,1)S(1)}, bf16[8,256,256]{2,1,0:T(8,128)(2,1)}, u32[]{:S(2)}) copy-start(bf16[8,256,256]{2,1,0:T(8,128)(2,1)} %shard_map.59) | copy-start | bytes 3145732
  24.9 11.1 %collective-permute-start.4 = (bf16[4,256,256]{2,1,0:T(8,128)(2,1)S(1)}, bf16[4,256,256]{2,1,0:T(8,128)(2,1)S(1)}, u32[]{:S(2)}, u32[]{:S(2)}) collective-permute-start(bf16[4,256,256]{2,1,0:T(8,128)(2,1)S(1)} %add_convert_fusion), channel_id=1, source_target_pairs={{0,2},{1,7},{2,0},{3,5},{4,6},{5,3},{6,4},{7,1},{8,10},{9,15},{10,... | collective-permute-start | bytes 1572872 | tf_op jit(solution)/shard_map/ppermute | solution.py:121
  29.7 16.9 %collective-permute-start.1 = (bf16[4,256,256]{2,1,0:T(8,128)(2,1)}, bf16[4,256,256]{2,1,0:T(8,128)(2,1)}, u32[]{:S(2)}, u32[]{:S(2)}) collective-permute-start(bf16[4,256,256]{2,1,0:T(8,128)(2,1)} %add_convert_fusion.1), channel_id=1, source_target_pairs={{0,2},{1,7},{2,0},{3,5},{4,6},{5,3},{6,4},{7,1},{8,10},{9,15},{10,... | collective-permute-start | bytes 1572872 | tf_op jit(solution)/shard_map/ppermute | solution.py:121
  36.0 9.7 %copy-start.3 = (bf16[4,256,256]{2,1,0:T(8,128)(2,1)}, bf16[4,256,256]{2,1,0:T(8,128)(2,1)S(1)}, u32[]{:S(2)}) copy-start(bf16[4,256,256]{2,1,0:T(8,128)(2,1)S(1)} %collective-permute-done.4) | copy-start | bytes 1572868
  37.9 12.6 %collective-permute-start.5 = (bf16[2,256,256]{2,1,0:T(8,128)(2,1)}, bf16[2,256,256]{2,1,0:T(8,128)(2,1)}, u32[]{:S(2)}, u32[]{:S(2)}) collective-permute-start(bf16[2,256,256]{2,1,0:T(8,128)(2,1)} %add_convert_fusion.3), channel_id=1, source_target_pairs={{0,6},{1,3},{2,4},{3,1},{4,2},{5,7},{6,0},{7,5},{8,14},{9,11},{10,... | collective-permute-start | bytes 786440 | tf_op jit(solution)/shard_map/ppermute | solution.py:121
  45.9 33.0 %copy-start.2 = (f32[64,256]{1,0:T(8,128)}, f32[64,256]{1,0:T(8,128)S(1)}, u32[]{:S(2)}) copy-start(f32[64,256]{1,0:T(8,128)S(1)} %mul.87.wide_ref) | copy-start | bytes 196612
  47.7 13.9 %collective-permute-start.2 = (bf16[2,256,256]{2,1,0:T(8,128)(2,1)S(1)}, bf16[2,256,256]{2,1,0:T(8,128)(2,1)S(1)}, u32[]{:S(2)}, u32[]{:S(2)}) collective-permute-start(bf16[2,256,256]{2,1,0:T(8,128)(2,1)S(1)} %add_convert_fusion.5), channel_id=1, source_target_pairs={{0,6},{1,3},{2,4},{3,1},{4,2},{5,7},{6,0},{7,5},{8,14},{9,11},{10,... | collective-permute-start | bytes 786440 | tf_op jit(solution)/shard_map/ppermute | solution.py:121
  51.8 13.5 %collective-permute-start.7 = (bf16[256,256]{1,0:T(8,128)(2,1)S(1)}, bf16[256,256]{1,0:T(8,128)(2,1)S(1)}, u32[]{:S(2)}, u32[]{:S(2)}) collective-permute-start(bf16[256,256]{1,0:T(8,128)(2,1)S(1)} %get-tuple-element.6), channel_id=1, source_target_pairs={{0,8},{1,25},{2,10},{3,27},{4,12},{5,29},{6,14},{7,31},{8,0},{9,17... | collective-permute-start | bytes 393224 | tf_op jit(solution)/shard_map/ppermute | solution.py:121
  58.1 15.4 %collective-permute-start.6 = (bf16[256,256]{1,0:T(8,128)(2,1)S(1)}, bf16[256,256]{1,0:T(8,128)(2,1)S(1)}, u32[]{:S(2)}, u32[]{:S(2)}) collective-permute-start(bf16[256,256]{1,0:T(8,128)(2,1)S(1)} %get-tuple-element.7), channel_id=1, source_target_pairs={{0,8},{1,25},{2,10},{3,27},{4,12},{5,29},{6,14},{7,31},{8,0},{9,17... | collective-permute-start | bytes 393224 | tf_op jit(solution)/shard_map/ppermute | solution.py:121
  65.3 13.5 %collective-permute-start.8 = (bf16[256,256]{1,0:T(8,128)(2,1)S(1)}, bf16[256,256]{1,0:T(8,128)(2,1)S(1)}, u32[]{:S(2)}, u32[]{:S(2)}) collective-permute-start(bf16[256,256]{1,0:T(8,128)(2,1)S(1)} %fusion), channel_id=1, source_target_pairs={{0,24},{1,9},{2,26},{3,11},{4,28},{5,13},{6,30},{7,15},{8,16},{9,1... | collective-permute-start | bytes 393224 | tf_op jit(solution)/shard_map/ppermute | solution.py:121
  73.5 5.4 %copy-start.4 = (bf16[256,256]{1,0:T(8,128)(2,1)}, bf16[256,256]{1,0:T(8,128)(2,1)S(1)}, u32[]{:S(2)}) copy-start(bf16[256,256]{1,0:T(8,128)(2,1)S(1)} %collective-permute-done.6.r1_ref) | copy-start | bytes 393220
  78.9 0.7 copy-start.5

commit v2 on v1

v2 whole, which is shorter than its diff:
```python
import functools
import math

import jax
import jax.numpy as jnp
from jax import lax
from jax.experimental import pallas as pl
from jax.experimental.pallas import tpu as pltpu
from jax.sharding import PartitionSpec as P

SPAN = 64
KEEP = 16
UNIT = 256
RING = 4
VMEM_LIMIT = 8 << 20
HIGH = lax.Precision.HIGHEST
BF16 = jnp.bfloat16
F32 = jnp.float32

MASKS = ((0, 3, 1, 2), (0, 1, 3, 2))

EARLY = tuple((p, q) for p in range(RING) for q in (2, 3))
LATE = tuple((p, q) for p in range(RING) for q in (0, 1))


def pairs(step):
    out = []
    for zh in range(RING):
        for x in range(RING):
            for c in range(2):
                a, b, d = step(zh, x, c)
                out.append(((zh * RING + x) * 2 + c, (a * RING + b) * 2 + d))
    return out


CORE = pairs(lambda zh, x, c: (zh, x, 1 - c))
X1 = pairs(lambda zh, x, c: (zh, x ^ MASKS[c][2], c))
X2 = pairs(lambda zh, x, c: (zh, x ^ MASKS[c][1], c))
Z1 = pairs(lambda zh, x, c: (zh ^ MASKS[c][2], x, c))
Z2 = pairs(lambda zh, x, c: (zh ^ MASKS[c][1], x, c))

LONG = pl.CostEstimate(flops=20_000_000_000, bytes_accessed=0, transcendentals=0)
IN_VMEM = pl.BlockSpec(memory_space=pltpu.VMEM)
PARAMS = pltpu.CompilerParams(vmem_limit_bytes=VMEM_LIMIT)


def block_start(me, flip, p, q):
    c = me % 2
    x = (me // 2) % RING
    zh = me // (2 * RING)
    if flip:
        c = 1 - c
    mx = jnp.where(c == 0, MASKS[0][p], MASKS[1][p])
    mz = jnp.where(c == 0, MASKS[0][q], MASKS[1][q])
    return pl.multiple_of((((zh ^ mz) * RING + (x ^ mx)) * 2 + c) * UNIT, UNIT)


def times(left, right):
    return jnp.dot(left, right, preferred_element_type=F32).astype(BF16)


def first_kernel(places, me_ref, tokens_ref, hidden_ref, out_ref, held_ref, left_ref, hidden, sems, hidden_sem):
    of_hidden = pltpu.make_async_copy(hidden_ref, hidden, hidden_sem)
    of_hidden.start()
    copies = []
    n = sems.shape[0]
    rows = tokens_ref.shape[0] // n
    for i in range(n):
        part = pl.ds(i * rows, rows)
        copy = pltpu.make_async_copy(tokens_ref.at[part], held_ref.at[part], sems.at[i])
        copy.start()
        copies.append(copy)
    of_hidden.wait()
    left = hidden[...].T
    left_ref[...] = left
    for copy in copies:
        copy.wait()
    for u, place in enumerate(places):
        out_ref[u] = times(left, held_ref[:, pl.ds(block_start(me_ref[0], *place), UNIT)])


def first_product(places, me, tokens, grad_hidden):
    toks, cols = grad_hidden.shape
    tokens = pltpu.with_memory_space_constraint(tokens, pltpu.HBM)
    grad_hidden = pltpu.with_memory_space_constraint(grad_hidden, pltpu.HBM)
    hbm = pl.BlockSpec(memory_space=pltpu.HBM)
    return pl.pallas_call(
        functools.partial(first_kernel, places),
        out_shape=(
            pltpu.VMEM((len(places), cols, UNIT), BF16),
            pltpu.VMEM(tokens.shape, BF16),
            pltpu.VMEM((cols, toks), BF16),
        ),
        in_specs=[pl.BlockSpec(memory_space=pltpu.SMEM), hbm, hbm],
        out_specs=(IN_VMEM, IN_VMEM, IN_VMEM),
        scratch_shapes=[
            pltpu.VMEM((toks, cols), BF16),
            pltpu.SemaphoreType.DMA((4,)),
            pltpu.SemaphoreType.DMA,
        ],
        compiler_params=PARAMS,
    )(me, tokens, grad_hidden)


def product_kernel(places, me_ref, left_ref, held_ref, out_ref):
    left = left_ref[...]
    for u, place in enumerate(places):
        out_ref[u] = times(left, held_ref[:, pl.ds(block_start(me_ref[0], *place), UNIT)])


def product(places, me, left, held, cost=None):
    cols, toks = left.shape
    return pl.pallas_call(
        functools.partial(product_kernel, places),
        out_shape=pltpu.VMEM((len(places), cols, UNIT), BF16),
        in_specs=[pl.BlockSpec(memory_space=pltpu.SMEM), IN_VMEM, IN_VMEM],
        out_specs=IN_VMEM,
        compiler_params=PARAMS,
        cost_estimate=cost,
    )(me, left, held)


def add_kernel(cuts, a_ref, b_ref, *out_refs):
    at = 0
    for out_ref, n in zip(out_refs, cuts, strict=True):
        for u in range(n):
            out_ref[u] = (a_ref[at + u].astype(F32) + b_ref[at + u].astype(F32)).astype(BF16)
        at += n


def add(a, b, *cuts, cost=None):
    return pl.pallas_call(
        functools.partial(add_kernel, cuts),
        out_shape=tuple(pltpu.VMEM((n, *a.shape[1:]), BF16) for n in cuts),
        in_specs=[IN_VMEM, IN_VMEM],
        out_specs=tuple(IN_VMEM for _ in cuts),
        compiler_params=PARAMS,
        cost_estimate=cost,
    )(a, b)


def kept_basis(kept):
    freq = kept.astype(F32)[:, None]
    place = jnp.arange(SPAN).astype(F32)[None, :]
    scale = jnp.where(kept == 0, math.sqrt(1.0 / SPAN), math.sqrt(2.0 / SPAN)).astype(F32)
    return scale[:, None] * jnp.cos(math.pi * (2.0 * place + 1.0) * freq / (2.0 * SPAN))


def dot(a, b):
    return jnp.dot(a, b, precision=HIGH, preferred_element_type=F32)


def block_basis(basis, blocks):
    k, n = basis.shape
    wide = jnp.concatenate([jnp.concatenate([basis] * blocks, axis=1)] * blocks, axis=0)
    row = lax.broadcasted_iota(jnp.int32, wide.shape, 0) // k
    col = lax.broadcasted_iota(jnp.int32, wide.shape, 1) // n
    return jnp.where(row == col, wide, 0.0)


def moment_kernel(part_ref, r1_ref, r2_ref, momentum_ref, basis_ref, moment_ref, coeffs_ref, sent_ref):
    grad = part_ref[0].astype(F32) + r1_ref[0].astype(F32) + r2_ref[0].astype(F32)
    moment = 0.9 * momentum_ref[0] + grad.T
    wide = block_basis(basis_ref[...], moment.shape[0] // SPAN)
    coeffs = dot(dot(wide, moment), wide.T)
    half = coeffs.shape[0] // 2
    sent = jnp.concatenate([coeffs[:half], coeffs[half:]], axis=1).astype(BF16)
    for r in range(sent_ref.shape[0]):
        sent_ref[r] = sent
    moment_ref[...] = moment
    coeffs_ref[...] = coeffs


def update_kernel(every_ref, moment_ref, coeffs_ref, basis_ref, out_ref, update_ref):
    total = jnp.sum(every_ref[...].astype(F32), axis=0)
    n = total.shape[1] // 2
    mean = jnp.concatenate([total[:, :n], total[:, n:]], axis=0) * (4.0 / every_ref.shape[0])
    wide = block_basis(basis_ref[...], out_ref.shape[1] // SPAN)
    tall = wide.T
    update_ref[...] = dot(tall, dot(mean, wide))
    out_ref[0] = moment_ref[...] - dot(tall, dot(coeffs_ref[...], wide))


def after(a, *others):
    return lax.optimization_barrier((a, *others))[0]


def on_device(tokens, grad_hidden, momentum, kept):
    rows = momentum.shape[1]
    cols = momentum.shape[2]
    n_dp = lax.axis_size("dp")
    me = lax.axis_index("fsdp").astype(jnp.int32).reshape(1)

    def swap(a, perm):
        return lax.ppermute(a, "fsdp", perm)

    def places(flip, group):
        return tuple((flip, p, q) for p, q in group)

    other_a, held, left = first_product(places(True, EARLY), me, tokens, grad_hidden)
    got_a = swap(other_a, CORE)
    own_a = product(places(False, EARLY), me, left, held)
    near, away = add(own_a, got_a, 4, 4)
    back = swap(away, X1)
    left_b = after(left, away)
    got_b = swap(product(places(True, LATE), me, left_b, held, LONG), CORE)
    own_b = product(places(False, LATE), me, left_b, held, LONG)
    near, away = add(near, back, 2, 2)
    first_away = away
    a2, a3 = add(near, swap(away, X2), 1, 1, cost=LONG)
    near, away = add(own_b, after(got_b, first_away), 4, 4)
    near, away = add(near, swap(away, X1), 2, 2)
    r3 = swap(a3, Z1)
    r2 = swap(after(a2, away), Z1)
    b0, b1 = add(near, swap(away, X2), 1, 1)
    (b1,) = add(b1, r3, 1)
    r1 = swap(b1, Z2)

    basis = kept_basis(kept)
    kw = cols // SPAN * KEEP
    moment, coeffs, sent = pl.pallas_call(
        moment_kernel,
        out_shape=(
            pltpu.VMEM((rows, cols), F32),
            pltpu.VMEM((kw, kw), F32),
            pltpu.VMEM((n_dp, kw // 2, kw * 2), BF16),
        ),
        in_specs=[IN_VMEM] * 5,
        out_specs=(IN_VMEM,) * 3,
        compiler_params=PARAMS,
    )(b0, r2, r1, momentum, basis)
    every = lax.all_to_all(sent, "dp", 0, 0, tiled=True)
    return pl.pallas_call(
        update_kernel,
        out_shape=(jax.ShapeDtypeStruct((1, rows, cols), F32), jax.ShapeDtypeStruct((rows, cols), F32)),
        in_specs=[IN_VMEM] * 4,
        out_specs=(IN_VMEM,) * 2,
        compiler_params=PARAMS,
    )(every, moment, coeffs, basis)


def solution(mesh):
    in_specs = (P(("dp", "fsdp"), None), P(("dp", "fsdp"), None), P("dp", "fsdp", None), P())
    out_specs = (P("dp", "fsdp", None), P("fsdp", None))
    return jax.shard_map(
        on_device, mesh=mesh, in_specs=in_specs, out_specs=out_specs, check_vma=False
    )
```

time: 105 us -> 83.3 us (0.79)
  Pallas kernels: 24.1 us -> 7.36 us
  other arithmetic: 8.76 us -> 0.13 us
  starting transfers between devices: 38 us -> 45.5 us
  local copies, waits for them, and re-layouts: 2.23 us -> 0.01 us
  blocking collectives: 18.6 us -> 17.1 us
    pallas_call x6 -> x13, Pallas kernels: 24.1 us -> 7.36 us  [the longest x1 2.71 us: first_product(): pl.pallas_call(functools.partial(first_kernel, places), out_shape=(pltpu....]
    convert_element_type x8 -> x0, other arithmetic: 8.53 us -> none  [the longest x7 8.53 us: add(): return (a.astype(F32) + b.astype(F32)).astype(BF16)]
    ppermute x9, starting transfers between devices: 38 us -> 45.5 us  [swap(): return lax.ppermute(a, 'fsdp', perm)]
    all_to_all x1, blocking collectives: 18.6 us -> 17.1 us  [on_device(): every = lax.all_to_all(sent, 'dp', 0, 0, tiled=True)]
  transfers between devices with their start and end apart: 9 -> 9, of which waited for: 3 -> 5; matrix products, arithmetic and copies ran while one was open for 10% -> 0% of each run, Pallas kernels for 13% -> 2%
where the time goes in v2:
time: 83.3 us; the launch traced here: 82.9 us
  starting transfers between devices  45.5 us (55%)
  blocking collectives  17.1 us (21%)
  waiting for transfers between devices  12 us (14%)
  Pallas kernels  7.36 us (9%)
  between operations  0.84 us (1%)
    ppermute x9, starting transfers between devices, swap(): return lax.ppermute(a, 'fsdp', perm)  45.5 us
    all_to_all x1, blocking collectives, on_device(): every = lax.all_to_all(sent, 'dp', 0, 0, tiled=True)  17.1 us
    ppermute x9, waiting for transfers between devices, swap(): return lax.ppermute(a, 'fsdp', perm)  12 us
    pallas_call x1, Pallas kernels, first_product(): pl.pallas_call(functools.partial(first_kernel, places), out_shape=(pltpu....  2.71 us
  transfers between devices with their start and end apart: 9, of which 5 were waited for; matrix products, arithmetic and copies ran while one was open for 0% of the time, Pallas kernels for 2%

profile of v2, /device:TPU:6, one launch (start us, length us, event | category | flops | bytes accessed | tf_op | source)
XLA Modules:
  0.0 82.9 jit_solution(579465429237755694)
XLA Ops:
  0.6 2.7 %shard_map.59 = (bf16[8,256,256]{2,1,0:T(8,128)(2,1)S(1)}, bf16[256,8192]{1,0:T(8,128)(2,1)S(1)}, bf16[256,256]{1,0:T(8,128)(2,1)S(1)}) custom-call(s32[1]{0:T(128)} %bitcast.me_ref, bf16[256,8192]{1,0:T(8,128)(2,1)} %tokens_ref.1, bf16[256,256]{1,0:T(8,128)(2,1)} %hidden_ref.1), custom_call_target="tpu_custom_call" | custom-call | tf_op jit(solution)/shard_map/pallas_call | solution.py:87
  3.3 1.9 %collective-permute-start = (bf16[8,256,256]{2,1,0:T(8,128)(2,1)S(1)}, bf16[8,256,256]{2,1,0:T(8,128)(2,1)S(1)}, u32[]{:S(2)}, u32[]{:S(2)}) collective-permute-start(bf16[8,256,256]{2,1,0:T(8,128)(2,1)S(1)} %get-tuple-element.25), channel_id=1, source_target_pairs={{0,1},{1,0},{2,3},{3,2},{4,5},{5,4},{6,7},{7,6},{8,9},{9,8},{10,11... | collective-permute-start | bytes 3145736 | tf_op jit(solution)/shard_map/ppermute | solution.py:195
  5.3 0.5 shard_map.60.a_ref
  5.8 2.1 %collective-permute-done.b_ref = bf16[8,256,256]{2,1,0:T(8,128)(2,1)S(1)} collective-permute-done((bf16[8,256,256]{2,1,0:T(8,128)(2,1)S(1)}, bf16[8,256,256]{2,1,0:T(8,128)(2,1)S(1)}, u32[]{:S(2)}, u32[]{:S(2)}) %collective-permute-start) | collective-permute-done | bytes 1048608 | tf_op jit(solution)/shard_map/ppermute | solution.py:195
  7.9 0.2 shard_map.61
  8.1 2.7 %collective-permute-start.2 = (bf16[4,256,256]{2,1,0:T(8,128)(2,1)S(1)}, bf16[4,256,256]{2,1,0:T(8,128)(2,1)S(1)}, u32[]{:S(2)}, u32[]{:S(2)}) collective-permute-start(bf16[4,256,256]{2,1,0:T(8,128)(2,1)S(1)} %get-tuple-element.26), channel_id=1, source_target_pairs={{0,2},{1,7},{2,0},{3,5},{4,6},{5,3},{6,4},{7,1},{8,10},{9,15},{10,... | collective-permute-start | bytes 1572872 | tf_op jit(solution)/shard_map/ppermute | solution.py:195
  10.9 0.5 shard_map.63
  11.4 6.8 %collective-permute-start.1 = (bf16[8,256,256]{2,1,0:T(8,128)(2,1)S(1)}, bf16[8,256,256]{2,1,0:T(8,128)(2,1)S(1)}, u32[]{:S(2)}, u32[]{:S(2)}) collective-permute-start(bf16[8,256,256]{2,1,0:T(8,128)(2,1)S(1)} %shard_map.63), channel_id=1, source_target_pairs={{0,1},{1,0},{2,3},{3,2},{4,5},{5,4},{6,7},{7,6},{8,9},{9,8},{10,11... | collective-permute-start | bytes 3145736 | tf_op jit(solution)/shard_map/ppermute | solution.py:195
  18.2 1.1 %collective-permute-done.2.b_ref = bf16[4,256,256]{2,1,0:T(8,128)(2,1)S(1)} collective-permute-done((bf16[4,256,256]{2,1,0:T(8,128)(2,1)S(1)}, bf16[4,256,256]{2,1,0:T(8,128)(2,1)S(1)}, u32[]{:S(2)}, u32[]{:S(2)}) %collective-permute-start.2) | collective-permute-done | bytes 524320 | tf_op jit(solution)/shard_map/ppermute | solution.py:195
  19.2 0.1 shard_map.64
  19.3 7.8 %collective-permute-start.5 = (bf16[2,256,256]{2,1,0:T(8,128)(2,1)S(1)}, bf16[2,256,256]{2,1,0:T(8,128)(2,1)S(1)}, u32[]{:S(2)}, u32[]{:S(2)}) collective-permute-start(bf16[2,256,256]{2,1,0:T(8,128)(2,1)S(1)} %get-tuple-element.29), channel_id=1, source_target_pairs={{0,6},{1,3},{2,4},{3,1},{4,2},{5,7},{6,0},{7,5},{8,14},{9,11},{10,... | collective-permute-start | bytes 786440 | tf_op jit(solution)/shard_map/ppermute | solution.py:195
  27.1 0.5 shard_map.62.a_ref
  27.6 0.0 collective-permute-done.1.b_ref
  27.6 0.2 shard_map.65
  27.9 1.9 %collective-permute-start.3 = (bf16[4,256,256]{2,1,0:T(8,128)(2,1)S(1)}, bf16[4,256,256]{2,1,0:T(8,128)(2,1)S(1)}, u32[]{:S(2)}, u32[]{:S(2)}) collective-permute-start(bf16[4,256,256]{2,1,0:T(8,128)(2,1)S(1)} %get-tuple-element.32), channel_id=1, source_target_pairs={{0,2},{1,7},{2,0},{3,5},{4,6},{5,3},{6,4},{7,1},{8,10},{9,15},{10,... | collective-permute-start | bytes 1572872 | tf_op jit(solution)/shard_map/ppermute | solution.py:195
  29.8 2.2 %collective-permute-done.5.b_ref = bf16[2,256,256]{2,1,0:T(8,128)(2,1)S(1)} collective-permute-done((bf16[2,256,256]{2,1,0:T(8,128)(2,1)S(1)}, bf16[2,256,256]{2,1,0:T(8,128)(2,1)S(1)}, u32[]{:S(2)}, u32[]{:S(2)}) %collective-permute-start.5) | collective-permute-done | bytes 262176 | tf_op jit(solution)/shard_map/ppermute | solution.py:195
  32.0 0.0 copy-start.1
  32.0 0.0 copy-start
  32.0 0.1 shard_map.68
  32.1 6.9 %collective-permute-start.7 = (bf16[1,256,256]{2,1,0:T(8,128)(2,1)S(1)}, bf16[1,256,256]{2,1,0:T(8,128)(2,1)S(1)}, u32[]{:S(2)}, u32[]{:S(2)}) collective-permute-start(bf16[1,256,256]{2,1,0:T(8,128)(2,1)S(1)} %get-tuple-element.40), channel_id=1, source_target_pairs={{0,8},{1,25},{2,10},{3,27},{4,12},{5,29},{6,14},{7,31},{8,0},{9,17... | collective-permute-start | bytes 393224 | tf_op jit(solution)/shard_map/ppermute | solution.py:195
  39.0 0.0 collective-permute-done.3.b_ref
  39.0 0.1 shard_map.66
  39.1 2.1 %collective-permute-start.4 = (bf16[2,256,256]{2,1,0:T(8,128)(2,1)S(1)}, bf16[2,256,256]{2,1,0:T(8,128)(2,1)S(1)}, u32[]{:S(2)}, u32[]{:S(2)}) collective-permute-start(bf16[2,256,256]{2,1,0:T(8,128)(2,1)S(1)} %get-tuple-element.34), channel_id=1, source_target_pairs={{0,6},{1,3},{2,4},{3,1},{4,2},{5,7},{6,0},{7,5},{8,14},{9,11},{10,... | collective-permute-start | bytes 786440 | tf_op jit(solution)/shard_map/ppermute | solution.py:195
  41.2 0.0 copy-done.1
  41.3 6.3 %collective-permute-start.6 = (bf16[1,256,256]{2,1,0:T(8,128)(2,1)S(1)}, bf16[1,256,256]{2,1,0:T(8,128)(2,1)S(1)}, u32[]{:S(2)}, u32[]{:S(2)}) collective-permute-start(bf16[1,256,256]{2,1,0:T(8,128)(2,1)S(1)} %get-tuple-element.38), channel_id=1, source_target_pairs={{0,8},{1,25},{2,10},{3,27},{4,12},{5,29},{6,14},{7,31},{8,0},{9,17... | collective-permute-start | bytes 393224 | tf_op jit(solution)/shard_map/ppermute | solution.py:195
  47.6 1.0 %collective-permute-done.4.b_ref = bf16[2,256,256]{2,1,0:T(8,128)(2,1)S(1)} collective-permute-done((bf16[2,256,256]{2,1,0:T(8,128)(2,1)S(1)}, bf16[2,256,256]{2,1,0:T(8,128)(2,1)S(1)}, u32[]{:S(2)}, u32[]{:S(2)}) %collective-permute-start.4) | collective-permute-done | bytes 262176 | tf_op jit(solution)/shard_map/ppermute | solution.py:195
  48.6 0.1 shard_map.67
  48.6 0.0 collective-permute-done.7.b_ref
  48.7 9.1 %collective-permute-start.8 = (bf16[1,256,256]{2,1,0:T(8,128)(2,1)S(1)}, bf16[1,256,256]{2,1,0:T(8,128)(2,1)S(1)}, u32[]{:S(2)}, u32[]{:S(2)}) collective-permute-start(bf16[1,256,256]{2,1,0:T(8,128)(2,1)S(1)} %shard_map.69), channel_id=1, source_target_pairs={{0,24},{1,9},{2,26},{3,11},{4,28},{5,13},{6,30},{7,15},{8,16},{9,1... | collective-permute-start | bytes 393224 | tf_op jit(solution)/shard_map/ppermute | solution.py:195
  57.8 0.1 cosine_multiply_fusion.basis_ref
  57.9 0.0 collective-permute-done.6.r1_ref
  57.9 5.5 %collective-permute-done.8.r2_ref = bf16[1,256,256]{2,1,0:T(8,128)(2,1)S(1)} collective-permute-done((bf16[1,256,256]{2,1,0:T(8,128)(2,1)S(1)}, bf16[1,256,256]{2,1,0:T(8,128)(2,1)S(1)}, u32[]{:S(2)}, u32[]{:S(2)}) %collective-permute-start.8) | collective-permute-done | bytes 131104 | tf_op jit(solution)/shard_map/ppermute | solution.py:195
  63.5 0.0 copy-done
  63.5 0.7 shard_map.70
  64.2 17.1 %all_to_all.5.every_ref = bf16[16,32,128]{2,1,0:T(8,128)(2,1)S(1)} all-to-all(bf16[16,32,128]{2,1,0:T(8,128)(2,1)S(1)} %get-tuple-element.41), channel_id=1, replica_groups=mesh['dp'=16,'fsdp'=32] {'dp'}, dimensions={0} | all-to-all | bytes 262144 | tf_op jit(solution)/shard_map/all_to_all | solution.py:232
  81.2 1.6 %shard_map.71 = (f32[1,256,256]{2,1,0:T(8,128)}, f32[256,256]{1,0:T(8,128)}) custom-call(bf16[16,32,128]{2,1,0:T(8,128)(2,1)S(1)} %all_to_all.5.every_ref, f32[256,256]{1,0:T(8,128)S(1)} %get-tuple-element.42.moment_ref, f32[64,64]{1,0:T(8,128)S(1)} %get-tuple-element.43.coeffs_ref, f32[16,64]{1,0:T(8,128)S(1)} %cosine_multiply_fusion.basis_ref), custom_call_target="tpu_custom_call" | custom-call | tf_op jit(solution)/shard_map/pallas_call | solution.py:233
  (4 shorter events, 0.1 us)
Async XLA Ops:
  3.3 4.6 %collective-permute-start = (bf16[8,256,256]{2,1,0:T(8,128)(2,1)S(1)}, bf16[8,256,256]{2,1,0:T(8,128)(2,1)S(1)}, u32[]{:S(2)}, u32[]{:S(2)}) collective-permute-start(bf16[8,256,256]{2,1,0:T(8,128)(2,1)S(1)} %get-tuple-element.25), channel_id=1, source_target_pairs={{0,1},{1,0},{2,3},{3,2},{4,5},{5,4},{6,7},{7,6},{8,9},{9,8},{10,11... | collective-permute-start | bytes 3145736 | tf_op jit(solution)/shard_map/ppermute | solution.py:195
  8.1 11.1 %collective-permute-start.2 = (bf16[4,256,256]{2,1,0:T(8,128)(2,1)S(1)}, bf16[4,256,256]{2,1,0:T(8,128)(2,1)S(1)}, u32[]{:S(2)}, u32[]{:S(2)}) collective-permute-start(bf16[4,256,256]{2,1,0:T(8,128)(2,1)S(1)} %get-tuple-element.26), channel_id=1, source_target_pairs={{0,2},{1,7},{2,0},{3,5},{4,6},{5,3},{6,4},{7,1},{8,10},{9,15},{10,... | collective-permute-start | bytes 1572872 | tf_op jit(solution)/shard_map/ppermute | solution.py:195
  11.4 16.2 %collective-permute-start.1 = (bf16[8,256,256]{2,1,0:T(8,128)(2,1)S(1)}, bf16[8,256,256]{2,1,0:T(8,128)(2,1)S(1)}, u32[]{:S(2)}, u32[]{:S(2)}) collective-permute-start(bf16[8,256,256]{2,1,0:T(8,128)(2,1)S(1)} %shard_map.63), channel_id=1, source_target_pairs={{0,1},{1,0},{2,3},{3,2},{4,5},{5,4},{6,7},{7,6},{8,9},{9,8},{10,11... | collective-permute-start | bytes 3145736 | tf_op jit(solution)/shard_map/ppermute | solution.py:195
  19.3 12.7 %collective-permute-start.5 = (bf16[2,256,256]{2,1,0:T(8,128)(2,1)S(1)}, bf16[2,256,256]{2,1,0:T(8,128)(2,1)S(1)}, u32[]{:S(2)}, u32[]{:S(2)}) collective-permute-start(bf16[2,256,256]{2,1,0:T(8,128)(2,1)S(1)} %get-tuple-element.29), channel_id=1, source_target_pairs={{0,6},{1,3},{2,4},{3,1},{4,2},{5,7},{6,0},{7,5},{8,14},{9,11},{10,... | collective-permute-start | bytes 786440 | tf_op jit(solution)/shard_map/ppermute | solution.py:195
  27.9 11.1 %collective-permute-start.3 = (bf16[4,256,256]{2,1,0:T(8,128)(2,1)S(1)}, bf16[4,256,256]{2,1,0:T(8,128)(2,1)S(1)}, u32[]{:S(2)}, u32[]{:S(2)}) collective-permute-start(bf16[4,256,256]{2,1,0:T(8,128)(2,1)S(1)} %get-tuple-element.32), channel_id=1, source_target_pairs={{0,2},{1,7},{2,0},{3,5},{4,6},{5,3},{6,4},{7,1},{8,10},{9,15},{10,... | collective-permute-start | bytes 1572872 | tf_op jit(solution)/shard_map/ppermute | solution.py:195
  32.0 9.2 %copy-start.1 = (s32[16]{0:T(128)S(1)}, s32[16]{0:T(128)}, u32[]{:S(2)}) copy-start(s32[16]{0:T(128)} %param.7) | copy-start | bytes 196
  32.0 31.4 %copy-start = (f32[1,256,256]{2,1,0:T(8,128)S(1)}, f32[1,256,256]{2,1,0:T(8,128)}, u32[]{:S(2)}) copy-start(f32[1,256,256]{2,1,0:T(8,128)} %momentum_ref.1) | copy-start | bytes 786436
  32.1 16.6 %collective-permute-start.7 = (bf16[1,256,256]{2,1,0:T(8,128)(2,1)S(1)}, bf16[1,256,256]{2,1,0:T(8,128)(2,1)S(1)}, u32[]{:S(2)}, u32[]{:S(2)}) collective-permute-start(bf16[1,256,256]{2,1,0:T(8,128)(2,1)S(1)} %get-tuple-element.40), channel_id=1, source_target_pairs={{0,8},{1,25},{2,10},{3,27},{4,12},{5,29},{6,14},{7,31},{8,0},{9,17... | collective-permute-start | bytes 393224 | tf_op jit(solution)/shard_map/ppermute | solution.py:195
  39.1 9.5 %collective-permute-start.4 = (bf16[2,256,256]{2,1,0:T(8,128)(2,1)S(1)}, bf16[2,256,256]{2,1,0:T(8,128)(2,1)S(1)}, u32[]{:S(2)}, u32[]{:S(2)}) collective-permute-start(bf16[2,256,256]{2,1,0:T(8,128)(2,1)S(1)} %get-tuple-element.34), channel_id=1, source_target_pairs={{0,6},{1,3},{2,4},{3,1},{4,2},{5,7},{6,0},{7,5},{8,14},{9,11},{10,... | collective-permute-start | bytes 786440 | tf_op jit(solution)/shard_map/ppermute | solution.py:195
  41.3 16.7 %collective-permute-start.6 = (bf16[1,256,256]{2,1,0:T(8,128)(2,1)S(1)}, bf16[1,256,256]{2,1,0:T(8,128)(2,1)S(1)}, u32[]{:S(2)}, u32[]{:S(2)}) collective-permute-start(bf16[1,256,256]{2,1,0:T(8,128)(2,1)S(1)} %get-tuple-element.38), channel_id=1, source_target_pairs={{0,8},{1,25},{2,10},{3,27},{4,12},{5,29},{6,14},{7,31},{8,0},{9,17... | collective-permute-start | bytes 393224 | tf_op jit(solution)/shard_map/ppermute | solution.py:195
  48.7 14.8 %collective-permute-start.8 = (bf16[1,256,256]{2,1,0:T(8,128)(2,1)S(1)}, bf16[1,256,256]{2,1,0:T(8,128)(2,1)S(1)}, u32[]{:S(2)}, u32[]{:S(2)}) collective-permute-start(bf16[1,256,256]{2,1,0:T(8,128)(2,1)S(1)} %shard_map.69), channel_id=1, source_target_pairs={{0,24},{1,9},{2,26},{3,11},{4,28},{5,13},{6,30},{7,15},{8,16},{9,1... | collective-permute-start | bytes 393224 | tf_op jit(solution)/shard_map/ppermute | solution.py:195

commit v3 on v2

--- a/solution.py
+++ b/solution.py
@@ -19,8 +19,8 @@
 
 MASKS = ((0, 3, 1, 2), (0, 1, 3, 2))
 
-EARLY = tuple((p, q) for p in range(RING) for q in (2, 3))
-LATE = tuple((p, q) for p in range(RING) for q in (0, 1))
+FIRST = tuple((p, q) for p in (2, 3) for q in (2, 3))
+REST = tuple((p, q) for p in (0, 1) for q in (2, 3)) + tuple((p, q) for p in range(RING) for q in (0, 1))
 
 
 def pairs(step):
@@ -120,23 +120,28 @@
     )(me, left, held)
 
 
-def add_kernel(cuts, a_ref, b_ref, *out_refs):
+def add_kernel(offsets, cuts, *refs):
+    in_refs, out_refs = refs[: len(offsets)], refs[len(offsets) :]
     at = 0
     for out_ref, n in zip(out_refs, cuts, strict=True):
         for u in range(n):
-            out_ref[u] = (a_ref[at + u].astype(F32) + b_ref[at + u].astype(F32)).astype(BF16)
+            total = in_refs[0][offsets[0] + at + u].astype(F32)
+            for in_ref, offset in zip(in_refs[1:], offsets[1:], strict=True):
+                total += in_ref[offset + at + u].astype(F32)
+            out_ref[u] = total.astype(BF16)
         at += n
 
 
-def add(a, b, *cuts, cost=None):
-    return pl.pallas_call(
-        functools.partial(add_kernel, cuts),
-        out_shape=tuple(pltpu.VMEM((n, *a.shape[1:]), BF16) for n in cuts),
-        in_specs=[IN_VMEM, IN_VMEM],
+def add(terms, cuts, cost=None):
+    arrays, offsets = zip(*terms, strict=True)
+    return pl.pallas_call(
+        functools.partial(add_kernel, offsets, cuts),
+        out_shape=tuple(pltpu.VMEM((n, *arrays[0].shape[1:]), BF16) for n in cuts),
+        in_specs=[IN_VMEM] * len(arrays),
         out_specs=tuple(IN_VMEM for _ in cuts),
         compiler_params=PARAMS,
         cost_estimate=cost,
-    )(a, b)
+    )(*arrays)
 
 
 def kept_basis(kept):
@@ -158,27 +163,55 @@
     return jnp.where(row == col, wide, 0.0)
 
 
-def moment_kernel(part_ref, r1_ref, r2_ref, momentum_ref, basis_ref, moment_ref, coeffs_ref, sent_ref):
-    grad = part_ref[0].astype(F32) + r1_ref[0].astype(F32) + r2_ref[0].astype(F32)
-    moment = 0.9 * momentum_ref[0] + grad.T
-    wide = block_basis(basis_ref[...], moment.shape[0] // SPAN)
+def coeffs_of(basis, moment):
+    wide = block_basis(basis, moment.shape[0] // SPAN)
     coeffs = dot(dot(wide, moment), wide.T)
     half = coeffs.shape[0] // 2
-    sent = jnp.concatenate([coeffs[:half], coeffs[half:]], axis=1).astype(BF16)
+    return coeffs, jnp.concatenate([coeffs[:half], coeffs[half:]], axis=1)
+
+
+def late_kernel(near_ref, away_ref, back_ref, basis_ref, near_out_ref, coeffs_ref):
+    near_out_ref[0] = (near_ref[0].astype(F32) + back_ref[0].astype(F32)).astype(BF16)
+    away = (away_ref[0].astype(F32) + back_ref[1].astype(F32)).astype(BF16)
+    coeffs_ref[...] = coeffs_of(basis_ref[...], away.astype(F32).T)[1]
+
+
+def near_kernel(near_ref, back_ref, momentum_ref, basis_ref, moment_ref, coeffs_ref):
+    moment = 0.9 * momentum_ref[0] + (near_ref[0].astype(F32) + back_ref[0].astype(F32)).T
+    moment_ref[...] = moment
+    coeffs_ref[...] = coeffs_of(basis_ref[...], moment)[1]
+
+
+def sent_kernel(a_ref, b_ref, sent_ref):
+    sent = (a_ref[...] + b_ref[...]).astype(BF16)
     for r in range(sent_ref.shape[0]):
         sent_ref[r] = sent
-    moment_ref[...] = moment
-    coeffs_ref[...] = coeffs
-
-
-def update_kernel(every_ref, moment_ref, coeffs_ref, basis_ref, out_ref, update_ref):
+
+
+def new_kernel(moment_ref, back_ref, basis_ref, out_ref):
+    moment = moment_ref[...] + back_ref[0].astype(F32).T
+    basis = basis_ref[...]
+    wide = block_basis(basis, moment.shape[1] // SPAN)
+    out_ref[0] = moment - dot(wide.T, dot(coeffs_of(basis, moment)[0], wide))
+
+
+def update_kernel(every_ref, basis_ref, update_ref):
     total = jnp.sum(every_ref[...].astype(F32), axis=0)
     n = total.shape[1] // 2
     mean = jnp.concatenate([total[:, :n], total[:, n:]], axis=0) * (4.0 / every_ref.shape[0])
-    wide = block_basis(basis_ref[...], out_ref.shape[1] // SPAN)
-    tall = wide.T
-    update_ref[...] = dot(tall, dot(mean, wide))
-    out_ref[0] = moment_ref[...] - dot(tall, dot(coeffs_ref[...], wide))
+    wide = block_basis(basis_ref[...], update_ref.shape[1] // SPAN)
+    update_ref[...] = dot(wide.T, dot(mean, wide))
+
+
+def on_vmem(kernel, out_shape, *args, cost=None):
+    return pl.pallas_call(
+        kernel,
+        out_shape=out_shape,
+        in_specs=[IN_VMEM] * len(args),
+        out_specs=jax.tree.map(lambda _: IN_VMEM, out_shape),
+        compiler_params=PARAMS,
+        cost_estimate=cost,
+    )(*args)
 
 
 def after(a, *others):
@@ -197,46 +230,39 @@
     def places(flip, group):
         return tuple((flip, p, q) for p, q in group)
 
-    other_a, held, left = first_product(places(True, EARLY), me, tokens, grad_hidden)
-    got_a = swap(other_a, CORE)
-    own_a = product(places(False, EARLY), me, left, held)
-    near, away = add(own_a, got_a, 4, 4)
+    got, held, left = first_product(places(True, FIRST), me, tokens, grad_hidden)
+    got = swap(got, CORE)
+    own = product(places(False, FIRST), me, left, held)
+    (away,) = add([(own, 0), (got, 0)], (4,))
     back = swap(away, X1)
-    left_b = after(left, away)
-    got_b = swap(product(places(True, LATE), me, left_b, held, LONG), CORE)
-    own_b = product(places(False, LATE), me, left_b, held, LONG)
-    near, away = add(near, back, 2, 2)
-    first_away = away
-    a2, a3 = add(near, swap(away, X2), 1, 1, cost=LONG)
-    near, away = add(own_b, after(got_b, first_away), 4, 4)
-    near, away = add(near, swap(away, X1), 2, 2)
+    left = after(left, away)
+    got = swap(product(places(True, REST), me, left, held, LONG), CORE)
+    own = product(places(False, REST), me, left, held, LONG)
+    near, away = add([(own, 0), (got, 0), (back, 0)], (2, 2))
+    back = swap(away, X2)
+    (late_away,) = add([(own, 8), (after(got, away), 8)], (4,), LONG)
+    late_back = swap(late_away, X1)
+    a2, a3 = add([(near, 0), (back, 0)], (1, 1), LONG)
     r3 = swap(a3, Z1)
+    near, away = add([(own, 4), (got, 4), (after(late_back, a3), 0)], (2, 2))
+    late_back = swap(away, X2)
     r2 = swap(after(a2, away), Z1)
-    b0, b1 = add(near, swap(away, X2), 1, 1)
-    (b1,) = add(b1, r3, 1)
-    r1 = swap(b1, Z2)
+    (away,) = add([(near, 1), (r3, 0)], (1,), LONG)
 
     basis = kept_basis(kept)
     kw = cols // SPAN * KEEP
-    moment, coeffs, sent = pl.pallas_call(
-        moment_kernel,
-        out_shape=(
-            pltpu.VMEM((rows, cols), F32),
-            pltpu.VMEM((kw, kw), F32),
-            pltpu.VMEM((n_dp, kw // 2, kw * 2), BF16),
-        ),
-        in_specs=[IN_VMEM] * 5,
-        out_specs=(IN_VMEM,) * 3,
-        compiler_params=PARAMS,
-    )(b0, r2, r1, momentum, basis)
+    packed = pltpu.VMEM((kw // 2, kw * 2), F32)
+    unit = pltpu.VMEM(away.shape, BF16)
+    b0, coeffs1 = on_vmem(late_kernel, (unit, packed), near, away, late_back, basis)
+    (away,) = add([(away, 0), (after(late_back, coeffs1), 1)], (1,), LONG)
+    coeffs1 = swap(coeffs1, Z2)
+    moment, coeffs0 = on_vmem(near_kernel, (pltpu.VMEM((rows, cols), F32), packed), b0, r2, momentum, basis)
+    r1 = swap(away, Z2)
+    sent = on_vmem(sent_kernel, pltpu.VMEM((n_dp, kw // 2, kw * 2), BF16), coeffs0, coeffs1, cost=LONG)
     every = lax.all_to_all(sent, "dp", 0, 0, tiled=True)
-    return pl.pallas_call(
-        update_kernel,
-        out_shape=(jax.ShapeDtypeStruct((1, rows, cols), F32), jax.ShapeDtypeStruct((rows, cols), F32)),
-        in_specs=[IN_VMEM] * 4,
-        out_specs=(IN_VMEM,) * 2,
-        compiler_params=PARAMS,
-    )(every, moment, coeffs, basis)
+    new_momentum = on_vmem(new_kernel, jax.ShapeDtypeStruct((1, rows, cols), F32), moment, r1, basis, cost=LONG)
+    update = on_vmem(update_kernel, jax.ShapeDtypeStruct((rows, cols), F32), every, basis)
+    return new_momentum, update
 
 
 def solution(mesh):

time: 83.3 us -> 79.9 us (0.959)
  blocking collectives: 17.1 us -> 0 us
  starting transfers between devices: 45.5 us -> 52.2 us
  waiting for transfers between devices: 12 us -> 16.1 us
  Pallas kernels: 7.36 us -> 10.1 us
    all_to_all x1 -> x0, blocking collectives: 17.1 us -> none  [on_device(): every = lax.all_to_all(sent, 'dp', 0, 0, tiled=True)]
    all_to_all x0 -> x1, starting transfers between devices: none -> 6.76 us  [on_device(): every = lax.all_to_all(sent, 'dp', 0, 0, tiled=True)]
    all_to_all x0 -> x1, waiting for transfers between devices: none -> 3.88 us  [on_device(): every = lax.all_to_all(sent, 'dp', 0, 0, tiled=True)]
    pallas_call x9 -> x12, Pallas kernels: 3.23 us -> 6.04 us  [the longest x5 5.28 us: on_vmem(): pl.pallas_call(kernel, out_shape=out_shape, in_specs=[IN_VMEM] * len(args...]
    ppermute x9 -> x10, waiting for transfers between devices: 12 us -> 12.2 us  [swap(): return lax.ppermute(a, 'fsdp', perm)]
    ppermute x9 -> x10, starting transfers between devices: 45.5 us -> 45.4 us  [swap(): return lax.ppermute(a, 'fsdp', perm)]
  transfers between devices with their start and end apart: 9 -> 11, of which waited for: 5 -> 8; matrix products, arithmetic and copies ran while one was open for 0% -> 0% of each run, Pallas kernels for 2% -> 7%
where the time goes in v3:
time: 79.9 us; the launch traced here: 79.4 us
  starting transfers between devices  52.2 us (65%)
  waiting for transfers between devices  16.1 us (20%)
  Pallas kernels  10.1 us (13%)
  between operations  0.88 us (1%)
    ppermute x10, starting transfers between devices, swap(): return lax.ppermute(a, 'fsdp', perm)  45.4 us
    ppermute x10, waiting for transfers between devices, swap(): return lax.ppermute(a, 'fsdp', perm)  12.2 us
    all_to_all x1, starting transfers between devices, on_device(): every = lax.all_to_all(sent, 'dp', 0, 0, tiled=True)  6.76 us
    pallas_call x5, Pallas kernels, on_vmem(): pl.pallas_call(kernel, out_shape=out_shape, in_specs=[IN_VMEM] * len(args...  5.28 us
    all_to_all x1, waiting for transfers between devices, on_device(): every = lax.all_to_all(sent, 'dp', 0, 0, tiled=True)  3.88 us
    pallas_call x1, Pallas kernels, first_product(): pl.pallas_call(functools.partial(first_kernel, places), out_shape=(pltpu....  2.56 us
  transfers between devices with their start and end apart: 11, of which 8 were waited for; matrix products, arithmetic and copies ran while one was open for 0% of the time, Pallas kernels for 7%

profile of v3, /device:TPU:6, one launch (start us, length us, event | category | flops | bytes accessed | tf_op | source)
XLA Modules:
  0.0 79.4 jit_solution(4197989612429154796)
XLA Ops:
  0.6 0.0 copy-start.1
  0.6 2.6 %shard_map.59 = (bf16[4,256,256]{2,1,0:T(8,128)(2,1)S(1)}, bf16[256,8192]{1,0:T(8,128)(2,1)S(1)}, bf16[256,256]{1,0:T(8,128)(2,1)S(1)}) custom-call(s32[1]{0:T(128)} %bitcast.me_ref, bf16[256,8192]{1,0:T(8,128)(2,1)} %tokens_ref.1, bf16[256,256]{1,0:T(8,128)(2,1)} %hidden_ref.1), custom_call_target="tpu_custom_call" | custom-call | tf_op jit(solution)/shard_map/pallas_call | solution.py:87
  3.2 1.9 %collective-permute-start = (bf16[4,256,256]{2,1,0:T(8,128)(2,1)S(1)}, bf16[4,256,256]{2,1,0:T(8,128)(2,1)S(1)}, u32[]{:S(2)}, u32[]{:S(2)}) collective-permute-start(bf16[4,256,256]{2,1,0:T(8,128)(2,1)S(1)} %get-tuple-element.22), channel_id=1, source_target_pairs={{0,1},{1,0},{2,3},{3,2},{4,5},{5,4},{6,7},{7,6},{8,9},{9,8},{10,11... | collective-permute-start | bytes 1572872 | tf_op jit(solution)/shard_map/ppermute | solution.py:228
  5.1 0.0 copy-done.1
  5.2 0.3 shard_map.60.refs_0_
  5.5 1.5 %collective-permute-done.refs_1_ = bf16[4,256,256]{2,1,0:T(8,128)(2,1)S(1)} collective-permute-done((bf16[4,256,256]{2,1,0:T(8,128)(2,1)S(1)}, bf16[4,256,256]{2,1,0:T(8,128)(2,1)S(1)}, u32[]{:S(2)}, u32[]{:S(2)}) %collective-permute-start) | collective-permute-done | bytes 524320 | tf_op jit(solution)/shard_map/ppermute | solution.py:228
  7.0 0.1 shard_map.61
  7.1 2.7 %collective-permute-start.2 = (bf16[4,256,256]{2,1,0:T(8,128)(2,1)S(1)}, bf16[4,256,256]{2,1,0:T(8,128)(2,1)S(1)}, u32[]{:S(2)}, u32[]{:S(2)}) collective-permute-start(bf16[4,256,256]{2,1,0:T(8,128)(2,1)S(1)} %shard_map.61), channel_id=1, source_target_pairs={{0,2},{1,7},{2,0},{3,5},{4,6},{5,3},{6,4},{7,1},{8,10},{9,15},{10,... | collective-permute-start | bytes 1572872 | tf_op jit(solution)/shard_map/ppermute | solution.py:228
  9.9 0.6 shard_map.63
  10.5 6.8 %collective-permute-start.1 = (bf16[12,256,256]{2,1,0:T(8,128)(2,1)S(1)}, bf16[12,256,256]{2,1,0:T(8,128)(2,1)S(1)}, u32[]{:S(2)}, u32[]{:S(2)}) collective-permute-start(bf16[12,256,256]{2,1,0:T(8,128)(2,1)S(1)} %shard_map.63), channel_id=1, source_target_pairs={{0,1},{1,0},{2,3},{3,2},{4,5},{5,4},{6,7},{7,6},{8,9},{9,8},{10,11... | collective-permute-start | bytes 4718600 | tf_op jit(solution)/shard_map/ppermute | solution.py:228
  17.3 0.6 shard_map.62.refs_0_
  17.9 0.3 collective-permute-done.2.refs_2_
  18.2 2.1 %collective-permute-done.1.refs_1_ = bf16[12,256,256]{2,1,0:T(8,128)(2,1)S(1)} collective-permute-done((bf16[12,256,256]{2,1,0:T(8,128)(2,1)S(1)}, bf16[12,256,256]{2,1,0:T(8,128)(2,1)S(1)}, u32[]{:S(2)}, u32[]{:S(2)}) %collective-permute-start.1) | collective-permute-done | bytes 1572896 | tf_op jit(solution)/shard_map/ppermute | solution.py:228
  20.3 0.2 shard_map.64
  20.5 5.7 %collective-permute-start.4 = (bf16[2,256,256]{2,1,0:T(8,128)(2,1)S(1)}, bf16[2,256,256]{2,1,0:T(8,128)(2,1)S(1)}, u32[]{:S(2)}, u32[]{:S(2)}) collective-permute-start(bf16[2,256,256]{2,1,0:T(8,128)(2,1)S(1)} %get-tuple-element.24), channel_id=1, source_target_pairs={{0,6},{1,3},{2,4},{3,1},{4,2},{5,7},{6,0},{7,5},{8,14},{9,11},{10,... | collective-permute-start | bytes 786440 | tf_op jit(solution)/shard_map/ppermute | solution.py:228
  26.2 0.1 shard_map.65
  26.3 1.9 %collective-permute-start.3 = (bf16[4,256,256]{2,1,0:T(8,128)(2,1)S(1)}, bf16[4,256,256]{2,1,0:T(8,128)(2,1)S(1)}, u32[]{:S(2)}, u32[]{:S(2)}) collective-permute-start(bf16[4,256,256]{2,1,0:T(8,128)(2,1)S(1)} %shard_map.65), channel_id=1, source_target_pairs={{0,2},{1,7},{2,0},{3,5},{4,6},{5,3},{6,4},{7,1},{8,10},{9,15},{10,... | collective-permute-start | bytes 1572872 | tf_op jit(solution)/shard_map/ppermute | solution.py:228
  28.2 3.5 %collective-permute-done.4.refs_1_ = bf16[2,256,256]{2,1,0:T(8,128)(2,1)S(1)} collective-permute-done((bf16[2,256,256]{2,1,0:T(8,128)(2,1)S(1)}, bf16[2,256,256]{2,1,0:T(8,128)(2,1)S(1)}, u32[]{:S(2)}, u32[]{:S(2)}) %collective-permute-start.4) | collective-permute-done | bytes 262176 | tf_op jit(solution)/shard_map/ppermute | solution.py:228
  31.7 0.1 shard_map.66
  31.8 6.8 %collective-permute-start.5 = (bf16[1,256,256]{2,1,0:T(8,128)(2,1)S(1)}, bf16[1,256,256]{2,1,0:T(8,128)(2,1)S(1)}, u32[]{:S(2)}, u32[]{:S(2)}) collective-permute-start(bf16[1,256,256]{2,1,0:T(8,128)(2,1)S(1)} %get-tuple-element.27), channel_id=1, source_target_pairs={{0,8},{1,25},{2,10},{3,27},{4,12},{5,29},{6,14},{7,31},{8,0},{9,17... | collective-permute-start | bytes 393224 | tf_op jit(solution)/shard_map/ppermute | solution.py:228
  38.5 0.1 cosine_multiply_fusion.basis_ref
  38.7 0.0 collective-permute-done.3.refs_2_
  38.7 0.2 shard_map.67
  38.9 2.1 %collective-permute-start.6 = (bf16[2,256,256]{2,1,0:T(8,128)(2,1)S(1)}, bf16[2,256,256]{2,1,0:T(8,128)(2,1)S(1)}, u32[]{:S(2)}, u32[]{:S(2)}) collective-permute-start(bf16[2,256,256]{2,1,0:T(8,128)(2,1)S(1)} %get-tuple-element.30), channel_id=1, source_target_pairs={{0,6},{1,3},{2,4},{3,1},{4,2},{5,7},{6,0},{7,5},{8,14},{9,11},{10,... | collective-permute-start | bytes 786440 | tf_op jit(solution)/shard_map/ppermute | solution.py:228
  41.0 6.3 %collective-permute-start.7 = (bf16[1,256,256]{2,1,0:T(8,128)(2,1)S(1)}, bf16[1,256,256]{2,1,0:T(8,128)(2,1)S(1)}, u32[]{:S(2)}, u32[]{:S(2)}) collective-permute-start(bf16[1,256,256]{2,1,0:T(8,128)(2,1)S(1)} %get-tuple-element.33), channel_id=1, source_target_pairs={{0,8},{1,25},{2,10},{3,27},{4,12},{5,29},{6,14},{7,31},{8,0},{9,17... | collective-permute-start | bytes 393224 | tf_op jit(solution)/shard_map/ppermute | solution.py:228
  47.3 0.0 collective-permute-done.5.refs_1_
  47.4 1.0 %collective-permute-done.6.back_ref.refs_1_ = bf16[2,256,256]{2,1,0:T(8,128)(2,1)S(1)} collective-permute-done((bf16[2,256,256]{2,1,0:T(8,128)(2,1)S(1)}, bf16[2,256,256]{2,1,0:T(8,128)(2,1)S(1)}, u32[]{:S(2)}, u32[]{:S(2)}) %collective-permute-start.6) | collective-permute-done | bytes 262176 | tf_op jit(solution)/shard_map/ppermute | solution.py:228
  48.4 0.7 shard_map.69
  49.0 0.0 copy-start
  49.1 9.3 %collective-permute-start.9 = (f32[32,128]{1,0:T(8,128)S(1)}, f32[32,128]{1,0:T(8,128)S(1)}, u32[]{:S(2)}, u32[]{:S(2)}) collective-permute-start(f32[32,128]{1,0:T(8,128)S(1)} %get-tuple-element.35), channel_id=1, source_target_pairs={{0,24},{1,9},{2,26},{3,11},{4,28},{5,13},{6,30},{7,15},{8,16},{9,1... | collective-permute-start | bytes 49160 | tf_op jit(solution)/shard_map/ppermute | solution.py:228
  58.4 1.9 %collective-permute-start.8 = (bf16[1,256,256]{2,1,0:T(8,128)(2,1)S(1)}, bf16[1,256,256]{2,1,0:T(8,128)(2,1)S(1)}, u32[]{:S(2)}, u32[]{:S(2)}) collective-permute-start(bf16[1,256,256]{2,1,0:T(8,128)(2,1)S(1)} %shard_map.71), channel_id=1, source_target_pairs={{0,24},{1,9},{2,26},{3,11},{4,28},{5,13},{6,30},{7,15},{8,16},{9,1... | collective-permute-start | bytes 393224 | tf_op jit(solution)/shard_map/ppermute | solution.py:228
  60.3 0.0 collective-permute-done.7.back_ref
  60.3 0.0 copy-done
  60.3 0.6 shard_map.70
  61.0 0.7 collective-permute-done.9.b_ref
  61.7 0.7 shard_map.73
  62.3 6.8 %all-to-all-start = ((bf16[16,32,128]{2,1,0:T(8,128)(2,1)}), bf16[16,32,128]{2,1,0:T(8,128)(2,1)S(1)}, u32[]{:S(2)}, u32[]{:S(2)}) async-start(bf16[16,32,128]{2,1,0:T(8,128)(2,1)} %shard_map.73), calls=%async_computation | async-start | bytes 262144 | tf_op jit(solution)/shard_map/all_to_all | solution.py:262
  69.1 3.2 %collective-permute-done.8.back_ref = bf16[1,256,256]{2,1,0:T(8,128)(2,1)S(1)} collective-permute-done((bf16[1,256,256]{2,1,0:T(8,128)(2,1)S(1)}, bf16[1,256,256]{2,1,0:T(8,128)(2,1)S(1)}, u32[]{:S(2)}, u32[]{:S(2)}) %collective-permute-start.8) | collective-permute-done | bytes 131104 | tf_op jit(solution)/shard_map/ppermute | solution.py:228
  72.2 1.9 %shard_map.72 = f32[1,256,256]{2,1,0:T(8,128)} custom-call(f32[256,256]{1,0:T(8,128)S(1)} %get-tuple-element.34.moment_ref, bf16[1,256,256]{2,1,0:T(8,128)(2,1)S(1)} %collective-permute-done.8.back_ref, f32[16,64]{1,0:T(8,128)S(1)} %cosine_multiply_fusion.basis_ref), custom_call_target="tpu_custom_call" | custom-call | flops 20000000000 | tf_op jit(solution)/shard_map/pallas_call | solution.py:207
  74.1 3.9 %all-to-all-done.every_ref = bf16[16,32,128]{2,1,0:T(8,128)(2,1)S(1)} async-done(((bf16[16,32,128]{2,1,0:T(8,128)(2,1)}), bf16[16,32,128]{2,1,0:T(8,128)(2,1)S(1)}, u32[]{:S(2)}, u32[]{:S(2)}) %all-to-all-start) | async-done | bytes 131104 | tf_op jit(solution)/shard_map/all_to_all | solution.py:262
  78.0 1.4 %shard_map.74 = f32[256,256]{1,0:T(8,128)} custom-call(bf16[16,32,128]{2,1,0:T(8,128)(2,1)S(1)} %all-to-all-done.every_ref, f32[16,64]{1,0:T(8,128)S(1)} %cosine_multiply_fusion.basis_ref), custom_call_target="tpu_custom_call" | custom-call | tf_op jit(solution)/shard_map/pallas_call | solution.py:207
  (5 shorter events, 0.1 us)
Async XLA Ops:
  0.6 4.5 %copy-start.1 = (s32[16]{0:T(128)S(1)}, s32[16]{0:T(128)}, u32[]{:S(2)}) copy-start(s32[16]{0:T(128)} %param.7) | copy-start | bytes 196
  3.2 3.8 %collective-permute-start = (bf16[4,256,256]{2,1,0:T(8,128)(2,1)S(1)}, bf16[4,256,256]{2,1,0:T(8,128)(2,1)S(1)}, u32[]{:S(2)}, u32[]{:S(2)}) collective-permute-start(bf16[4,256,256]{2,1,0:T(8,128)(2,1)S(1)} %get-tuple-element.22), channel_id=1, source_target_pairs={{0,1},{1,0},{2,3},{3,2},{4,5},{5,4},{6,7},{7,6},{8,9},{9,8},{10,11... | collective-permute-start | bytes 1572872 | tf_op jit(solution)/shard_map/ppermute | solution.py:228
  7.1 11.1 %collective-permute-start.2 = (bf16[4,256,256]{2,1,0:T(8,128)(2,1)S(1)}, bf16[4,256,256]{2,1,0:T(8,128)(2,1)S(1)}, u32[]{:S(2)}, u32[]{:S(2)}) collective-permute-start(bf16[4,256,256]{2,1,0:T(8,128)(2,1)S(1)} %shard_map.61), channel_id=1, source_target_pairs={{0,2},{1,7},{2,0},{3,5},{4,6},{5,3},{6,4},{7,1},{8,10},{9,15},{10,... | collective-permute-start | bytes 1572872 | tf_op jit(solution)/shard_map/ppermute | solution.py:228
  10.5 9.8 %collective-permute-start.1 = (bf16[12,256,256]{2,1,0:T(8,128)(2,1)S(1)}, bf16[12,256,256]{2,1,0:T(8,128)(2,1)S(1)}, u32[]{:S(2)}, u32[]{:S(2)}) collective-permute-start(bf16[12,256,256]{2,1,0:T(8,128)(2,1)S(1)} %shard_map.63), channel_id=1, source_target_pairs={{0,1},{1,0},{2,3},{3,2},{4,5},{5,4},{6,7},{7,6},{8,9},{9,8},{10,11... | collective-permute-start | bytes 4718600 | tf_op jit(solution)/shard_map/ppermute | solution.py:228
  20.5 11.2 %collective-permute-start.4 = (bf16[2,256,256]{2,1,0:T(8,128)(2,1)S(1)}, bf16[2,256,256]{2,1,0:T(8,128)(2,1)S(1)}, u32[]{:S(2)}, u32[]{:S(2)}) collective-permute-start(bf16[2,256,256]{2,1,0:T(8,128)(2,1)S(1)} %get-tuple-element.24), channel_id=1, source_target_pairs={{0,6},{1,3},{2,4},{3,1},{4,2},{5,7},{6,0},{7,5},{8,14},{9,11},{10,... | collective-permute-start | bytes 786440 | tf_op jit(solution)/shard_map/ppermute | solution.py:228
  26.3 12.4 %collective-permute-start.3 = (bf16[4,256,256]{2,1,0:T(8,128)(2,1)S(1)}, bf16[4,256,256]{2,1,0:T(8,128)(2,1)S(1)}, u32[]{:S(2)}, u32[]{:S(2)}) collective-permute-start(bf16[4,256,256]{2,1,0:T(8,128)(2,1)S(1)} %shard_map.65), channel_id=1, source_target_pairs={{0,2},{1,7},{2,0},{3,5},{4,6},{5,3},{6,4},{7,1},{8,10},{9,15},{10,... | collective-permute-start | bytes 1572872 | tf_op jit(solution)/shard_map/ppermute | solution.py:228
  31.8 15.6 %collective-permute-start.5 = (bf16[1,256,256]{2,1,0:T(8,128)(2,1)S(1)}, bf16[1,256,256]{2,1,0:T(8,128)(2,1)S(1)}, u32[]{:S(2)}, u32[]{:S(2)}) collective-permute-start(bf16[1,256,256]{2,1,0:T(8,128)(2,1)S(1)} %get-tuple-element.27), channel_id=1, source_target_pairs={{0,8},{1,25},{2,10},{3,27},{4,12},{5,29},{6,14},{7,31},{8,0},{9,17... | collective-permute-start | bytes 393224 | tf_op jit(solution)/shard_map/ppermute | solution.py:228
  38.9 9.5 %collective-permute-start.6 = (bf16[2,256,256]{2,1,0:T(8,128)(2,1)S(1)}, bf16[2,256,256]{2,1,0:T(8,128)(2,1)S(1)}, u32[]{:S(2)}, u32[]{:S(2)}) collective-permute-start(bf16[2,256,256]{2,1,0:T(8,128)(2,1)S(1)} %get-tuple-element.30), channel_id=1, source_target_pairs={{0,6},{1,3},{2,4},{3,1},{4,2},{5,7},{6,0},{7,5},{8,14},{9,11},{10,... | collective-permute-start | bytes 786440 | tf_op jit(solution)/shard_map/ppermute | solution.py:228
  41.0 19.3 %collective-permute-start.7 = (bf16[1,256,256]{2,1,0:T(8,128)(2,1)S(1)}, bf16[1,256,256]{2,1,0:T(8,128)(2,1)S(1)}, u32[]{:S(2)}, u32[]{:S(2)}) collective-permute-start(bf16[1,256,256]{2,1,0:T(8,128)(2,1)S(1)} %get-tuple-element.33), channel_id=1, source_target_pairs={{0,8},{1,25},{2,10},{3,27},{4,12},{5,29},{6,14},{7,31},{8,0},{9,17... | collective-permute-start | bytes 393224 | tf_op jit(solution)/shard_map/ppermute | solution.py:228
  49.0 11.3 %copy-start = (f32[1,256,256]{2,1,0:T(8,128)S(1)}, f32[1,256,256]{2,1,0:T(8,128)}, u32[]{:S(2)}) copy-start(f32[1,256,256]{2,1,0:T(8,128)} %momentum_ref.1) | copy-start | bytes 786436
  49.1 12.6 %collective-permute-start.9 = (f32[32,128]{1,0:T(8,128)S(1)}, f32[32,128]{1,0:T(8,128)S(1)}, u32[]{:S(2)}, u32[]{:S(2)}) collective-permute-start(f32[32,128]{1,0:T(8,128)S(1)} %get-tuple-element.35), channel_id=1, source_target_pairs={{0,24},{1,9},{2,26},{3,11},{4,28},{5,13},{6,30},{7,15},{8,16},{9,1... | collective-permute-start | bytes 49160 | tf_op jit(solution)/shard_map/ppermute | solution.py:228
  58.4 13.9 %collective-permute-start.8 = (bf16[1,256,256]{2,1,0:T(8,128)(2,1)S(1)}, bf16[1,256,256]{2,1,0:T(8,128)(2,1)S(1)}, u32[]{:S(2)}, u32[]{:S(2)}) collective-permute-start(bf16[1,256,256]{2,1,0:T(8,128)(2,1)S(1)} %shard_map.71), channel_id=1, source_target_pairs={{0,24},{1,9},{2,26},{3,11},{4,28},{5,13},{6,30},{7,15},{8,16},{9,1... | collective-permute-start | bytes 393224 | tf_op jit(solution)/shard_map/ppermute | solution.py:228
  62.3 15.7 %all-to-all-start = ((bf16[16,32,128]{2,1,0:T(8,128)(2,1)}), bf16[16,32,128]{2,1,0:T(8,128)(2,1)S(1)}, u32[]{:S(2)}, u32[]{:S(2)}) async-start(bf16[16,32,128]{2,1,0:T(8,128)(2,1)} %shard_map.73), calls=%async_computation | async-start | bytes 262144 | tf_op jit(solution)/shard_map/all_to_all | solution.py:262

commit v4 on v3

--- a/solution.py
+++ b/solution.py
@@ -19,8 +19,9 @@
 
 MASKS = ((0, 3, 1, 2), (0, 1, 3, 2))
 
-FIRST = tuple((p, q) for p in (2, 3) for q in (2, 3))
-REST = tuple((p, q) for p in (0, 1) for q in (2, 3)) + tuple((p, q) for p in range(RING) for q in (0, 1))
+EARLY = tuple((p, q) for p in (2, 3) for q in (3, 2))
+LATE = tuple((p, q) for p in (2, 3) for q in (0, 1))
+REST = tuple((p, q) for p in (0, 1) for q in (3, 2)) + tuple((p, q) for p in (0, 1) for q in (0, 1))
 
 
 def pairs(step):
@@ -230,23 +231,26 @@
     def places(flip, group):
         return tuple((flip, p, q) for p, q in group)
 
-    got, held, left = first_product(places(True, FIRST), me, tokens, grad_hidden)
+    got, held, left = first_product(places(True, EARLY + LATE), me, tokens, grad_hidden)
     got = swap(got, CORE)
-    own = product(places(False, FIRST), me, left, held)
-    (away,) = add([(own, 0), (got, 0)], (4,))
-    back = swap(away, X1)
-    left = after(left, away)
-    got = swap(product(places(True, REST), me, left, held, LONG), CORE)
-    own = product(places(False, REST), me, left, held, LONG)
-    near, away = add([(own, 0), (got, 0), (back, 0)], (2, 2))
-    back = swap(away, X2)
-    (late_away,) = add([(own, 8), (after(got, away), 8)], (4,), LONG)
+    own = product(places(False, EARLY + LATE), me, left, held)
+    (early_away,) = add([(own, 0), (got, 0)], (4,))
+    early_back = swap(early_away, X1)
+    left = after(left, early_away)
+    other = product(places(True, REST), me, left, held, LONG)
+    got_rest = swap(other, CORE)
+    (late_away,) = add([(own, 4), (after(got, other), 4)], (4,))
     late_back = swap(late_away, X1)
-    a2, a3 = add([(near, 0), (back, 0)], (1, 1), LONG)
+    own = product(places(False, REST), me, after(left, late_away), held, LONG)
+    near3, near2, away3, away2 = add([(own, 0), (got_rest, 0), (early_back, 0)], (1, 1, 1, 1))
+    back3 = swap(away3, X2)
+    back2 = swap(away2, X2)
+    (a3,) = add([(near3, 0), (back3, 0)], (1,))
     r3 = swap(a3, Z1)
-    near, away = add([(own, 4), (got, 4), (after(late_back, a3), 0)], (2, 2))
+    near, away = add([(own, 4), (got_rest, 4), (after(late_back, a3), 0)], (2, 2))
     late_back = swap(away, X2)
-    r2 = swap(after(a2, away), Z1)
+    (a2,) = add([(near2, 0), (after(back2, away), 0)], (1,))
+    r2 = swap(a2, Z1)
     (away,) = add([(near, 1), (r3, 0)], (1,), LONG)
 
     basis = kept_basis(kept)

time: 79.9 us -> 78.4 us (0.981)
  waiting for transfers between devices: 16.1 us -> 12 us
  starting transfers between devices: 52.2 us -> 54.6 us
    ppermute x10 -> x11, waiting for transfers between devices: 12.2 us -> 7.6 us  [swap(): return lax.ppermute(a, 'fsdp', perm)]
    ppermute x10 -> x11, starting transfers between devices: 45.4 us -> 46.7 us  [swap(): return lax.ppermute(a, 'fsdp', perm)]
    all_to_all x1, starting transfers between devices: 6.76 us -> 7.95 us  [on_device(): every = lax.all_to_all(sent, 'dp', 0, 0, tiled=True)]
  transfers between devices with their start and end apart: 11 -> 12, of which waited for: 8 -> 5; matrix products, arithmetic and copies ran while one was open for 0% -> 0% of each run, Pallas kernels for 7% -> 8%
where the time goes in v4:
time: 78.4 us; the launch traced here: 78 us
  starting transfers between devices  54.6 us (70%)
  waiting for transfers between devices  12 us (15%)
  Pallas kernels  10.2 us (13%)
  between operations  0.98 us (1%)
    ppermute x11, starting transfers between devices, swap(): return lax.ppermute(a, 'fsdp', perm)  46.7 us
    all_to_all x1, starting transfers between devices, on_device(): every = lax.all_to_all(sent, 'dp', 0, 0, tiled=True)  7.95 us
    ppermute x11, waiting for transfers between devices, swap(): return lax.ppermute(a, 'fsdp', perm)  7.6 us
    pallas_call x5, Pallas kernels, on_vmem(): pl.pallas_call(kernel, out_shape=out_shape, in_specs=[IN_VMEM] * len(args...  5.29 us
    all_to_all x1, waiting for transfers between devices, on_device(): every = lax.all_to_all(sent, 'dp', 0, 0, tiled=True)  4.41 us
    pallas_call x1, Pallas kernels, first_product(): pl.pallas_call(functools.partial(first_kernel, places), out_shape=(pltpu....  2.71 us
  transfers between devices with their start and end apart: 12, of which 5 were waited for; matrix products, arithmetic and copies ran while one was open for 0% of the time, Pallas kernels for 8%

profile of v4, /device:TPU:6, one launch (start us, length us, event | category | flops | bytes accessed | tf_op | source)
XLA Modules:
  0.0 78.0 jit_solution(9715871137834528694)
XLA Ops:
  0.6 2.7 %shard_map.59 = (bf16[8,256,256]{2,1,0:T(8,128)(2,1)S(1)}, bf16[256,8192]{1,0:T(8,128)(2,1)S(1)}, bf16[256,256]{1,0:T(8,128)(2,1)S(1)}) custom-call(s32[1]{0:T(128)} %bitcast.me_ref, bf16[256,8192]{1,0:T(8,128)(2,1)} %tokens_ref.1, bf16[256,256]{1,0:T(8,128)(2,1)} %hidden_ref.1), custom_call_target="tpu_custom_call" | custom-call | tf_op jit(solution)/shard_map/pallas_call | solution.py:88
  3.3 1.9 %collective-permute-start = (bf16[8,256,256]{2,1,0:T(8,128)(2,1)S(1)}, bf16[8,256,256]{2,1,0:T(8,128)(2,1)S(1)}, u32[]{:S(2)}, u32[]{:S(2)}) collective-permute-start(bf16[8,256,256]{2,1,0:T(8,128)(2,1)S(1)} %get-tuple-element.23), channel_id=1, source_target_pairs={{0,1},{1,0},{2,3},{3,2},{4,5},{5,4},{6,7},{7,6},{8,9},{9,8},{10,11... | collective-permute-start | bytes 3145736 | tf_op jit(solution)/shard_map/ppermute | solution.py:229
  5.3 0.5 shard_map.60.refs_0_
  5.8 2.1 %collective-permute-done.refs_1_ = bf16[8,256,256]{2,1,0:T(8,128)(2,1)S(1)} collective-permute-done((bf16[8,256,256]{2,1,0:T(8,128)(2,1)S(1)}, bf16[8,256,256]{2,1,0:T(8,128)(2,1)S(1)}, u32[]{:S(2)}, u32[]{:S(2)}) %collective-permute-start) | collective-permute-done | bytes 1048608 | tf_op jit(solution)/shard_map/ppermute | solution.py:229
  7.9 0.1 shard_map.61
  8.0 2.7 %collective-permute-start.3 = (bf16[4,256,256]{2,1,0:T(8,128)(2,1)S(1)}, bf16[4,256,256]{2,1,0:T(8,128)(2,1)S(1)}, u32[]{:S(2)}, u32[]{:S(2)}) collective-permute-start(bf16[4,256,256]{2,1,0:T(8,128)(2,1)S(1)} %shard_map.61), channel_id=1, source_target_pairs={{0,2},{1,7},{2,0},{3,5},{4,6},{5,3},{6,4},{7,1},{8,10},{9,15},{10,... | collective-permute-start | bytes 1572872 | tf_op jit(solution)/shard_map/ppermute | solution.py:229
  10.8 0.5 shard_map.62
  11.2 6.8 %collective-permute-start.1 = (bf16[8,256,256]{2,1,0:T(8,128)(2,1)S(1)}, bf16[8,256,256]{2,1,0:T(8,128)(2,1)S(1)}, u32[]{:S(2)}, u32[]{:S(2)}) collective-permute-start(bf16[8,256,256]{2,1,0:T(8,128)(2,1)S(1)} %shard_map.62), channel_id=1, source_target_pairs={{0,1},{1,0},{2,3},{3,2},{4,5},{5,4},{6,7},{7,6},{8,9},{9,8},{10,11... | collective-permute-start | bytes 3145736 | tf_op jit(solution)/shard_map/ppermute | solution.py:229
  18.0 0.1 shard_map.63
  18.2 0.0 copy-start.1
  18.2 1.9 %collective-permute-start.2 = (bf16[4,256,256]{2,1,0:T(8,128)(2,1)S(1)}, bf16[4,256,256]{2,1,0:T(8,128)(2,1)S(1)}, u32[]{:S(2)}, u32[]{:S(2)}) collective-permute-start(bf16[4,256,256]{2,1,0:T(8,128)(2,1)S(1)} %shard_map.63), channel_id=1, source_target_pairs={{0,2},{1,7},{2,0},{3,5},{4,6},{5,3},{6,4},{7,1},{8,10},{9,15},{10,... | collective-permute-start | bytes 1572872 | tf_op jit(solution)/shard_map/ppermute | solution.py:229
  20.1 0.5 shard_map.64.refs_0_
  20.6 0.0 collective-permute-done.3.refs_2_
  20.6 0.0 collective-permute-done.1.refs_1_
  20.6 0.2 shard_map.65
  20.8 6.3 %collective-permute-start.4 = (bf16[1,256,256]{2,1,0:T(8,128)(2,1)S(1)}, bf16[1,256,256]{2,1,0:T(8,128)(2,1)S(1)}, u32[]{:S(2)}, u32[]{:S(2)}) collective-permute-start(bf16[1,256,256]{2,1,0:T(8,128)(2,1)S(1)} %get-tuple-element.28), channel_id=1, source_target_pairs={{0,6},{1,3},{2,4},{3,1},{4,2},{5,7},{6,0},{7,5},{8,14},{9,11},{10,... | collective-permute-start | bytes 393224 | tf_op jit(solution)/shard_map/ppermute | solution.py:229
  27.1 0.0 copy-done.1
  27.1 1.9 %collective-permute-start.7 = (bf16[1,256,256]{2,1,0:T(8,128)(2,1)S(1)}, bf16[1,256,256]{2,1,0:T(8,128)(2,1)S(1)}, u32[]{:S(2)}, u32[]{:S(2)}) collective-permute-start(bf16[1,256,256]{2,1,0:T(8,128)(2,1)S(1)} %get-tuple-element.34), channel_id=1, source_target_pairs={{0,6},{1,3},{2,4},{3,1},{4,2},{5,7},{6,0},{7,5},{8,14},{9,11},{10,... | collective-permute-start | bytes 393224 | tf_op jit(solution)/shard_map/ppermute | solution.py:229
  29.0 1.9 %collective-permute-done.4.refs_1_ = bf16[1,256,256]{2,1,0:T(8,128)(2,1)S(1)} collective-permute-done((bf16[1,256,256]{2,1,0:T(8,128)(2,1)S(1)}, bf16[1,256,256]{2,1,0:T(8,128)(2,1)S(1)}, u32[]{:S(2)}, u32[]{:S(2)}) %collective-permute-start.4) | collective-permute-done | bytes 131104 | tf_op jit(solution)/shard_map/ppermute | solution.py:229
  30.9 5.6 %collective-permute-start.5 = (bf16[1,256,256]{2,1,0:T(8,128)(2,1)S(1)}, bf16[1,256,256]{2,1,0:T(8,128)(2,1)S(1)}, u32[]{:S(2)}, u32[]{:S(2)}) collective-permute-start(bf16[1,256,256]{2,1,0:T(8,128)(2,1)S(1)} %shard_map.66), channel_id=1, source_target_pairs={{0,8},{1,25},{2,10},{3,27},{4,12},{5,29},{6,14},{7,31},{8,0},{9,17... | collective-permute-start | bytes 393224 | tf_op jit(solution)/shard_map/ppermute | solution.py:229
  36.5 0.1 cosine_multiply_fusion.basis_ref
  36.6 0.0 collective-permute-done.2.refs_2_
  36.6 0.2 shard_map.67
  36.8 2.8 %collective-permute-start.6 = (bf16[2,256,256]{2,1,0:T(8,128)(2,1)S(1)}, bf16[2,256,256]{2,1,0:T(8,128)(2,1)S(1)}, u32[]{:S(2)}, u32[]{:S(2)}) collective-permute-start(bf16[2,256,256]{2,1,0:T(8,128)(2,1)S(1)} %get-tuple-element.31), channel_id=1, source_target_pairs={{0,6},{1,3},{2,4},{3,1},{4,2},{5,7},{6,0},{7,5},{8,14},{9,11},{10,... | collective-permute-start | bytes 786440 | tf_op jit(solution)/shard_map/ppermute | solution.py:229
  39.7 0.0 collective-permute-done.7.refs_1_
  39.7 5.6 %collective-permute-start.8 = (bf16[1,256,256]{2,1,0:T(8,128)(2,1)S(1)}, bf16[1,256,256]{2,1,0:T(8,128)(2,1)S(1)}, u32[]{:S(2)}, u32[]{:S(2)}) collective-permute-start(bf16[1,256,256]{2,1,0:T(8,128)(2,1)S(1)} %shard_map.70), channel_id=1, source_target_pairs={{0,8},{1,25},{2,10},{3,27},{4,12},{5,29},{6,14},{7,31},{8,0},{9,17... | collective-permute-start | bytes 393224 | tf_op jit(solution)/shard_map/ppermute | solution.py:229
  45.3 0.0 collective-permute-done.5.refs_1_
  45.4 0.9 %collective-permute-done.6.back_ref.refs_1_ = bf16[2,256,256]{2,1,0:T(8,128)(2,1)S(1)} collective-permute-done((bf16[2,256,256]{2,1,0:T(8,128)(2,1)S(1)}, bf16[2,256,256]{2,1,0:T(8,128)(2,1)S(1)}, u32[]{:S(2)}, u32[]{:S(2)}) %collective-permute-start.6) | collective-permute-done | bytes 262176 | tf_op jit(solution)/shard_map/ppermute | solution.py:229
  46.3 0.7 shard_map.69
  47.0 0.0 copy-start
  47.0 9.3 %collective-permute-start.10 = (f32[32,128]{1,0:T(8,128)S(1)}, f32[32,128]{1,0:T(8,128)S(1)}, u32[]{:S(2)}, u32[]{:S(2)}) collective-permute-start(f32[32,128]{1,0:T(8,128)S(1)} %get-tuple-element.37), channel_id=1, source_target_pairs={{0,24},{1,9},{2,26},{3,11},{4,28},{5,13},{6,30},{7,15},{8,16},{9,1... | collective-permute-start | bytes 49160 | tf_op jit(solution)/shard_map/ppermute | solution.py:229
  56.3 1.9 %collective-permute-start.9 = (bf16[1,256,256]{2,1,0:T(8,128)(2,1)S(1)}, bf16[1,256,256]{2,1,0:T(8,128)(2,1)S(1)}, u32[]{:S(2)}, u32[]{:S(2)}) collective-permute-start(bf16[1,256,256]{2,1,0:T(8,128)(2,1)S(1)} %shard_map.72), channel_id=1, source_target_pairs={{0,24},{1,9},{2,26},{3,11},{4,28},{5,13},{6,30},{7,15},{8,16},{9,1... | collective-permute-start | bytes 393224 | tf_op jit(solution)/shard_map/ppermute | solution.py:229
  58.3 0.0 collective-permute-done.8.back_ref
  58.3 0.0 copy-done
  58.3 0.6 shard_map.71
  59.0 0.0 collective-permute-done.10.b_ref
  59.0 0.7 shard_map.74
  59.7 7.9 %all-to-all-start = ((bf16[16,32,128]{2,1,0:T(8,128)(2,1)}), bf16[16,32,128]{2,1,0:T(8,128)(2,1)S(1)}, u32[]{:S(2)}, u32[]{:S(2)}) async-start(bf16[16,32,128]{2,1,0:T(8,128)(2,1)} %shard_map.74), calls=%async_computation | async-start | bytes 262144 | tf_op jit(solution)/shard_map/all_to_all | solution.py:266
  67.6 2.6 %collective-permute-done.9.back_ref = bf16[1,256,256]{2,1,0:T(8,128)(2,1)S(1)} collective-permute-done((bf16[1,256,256]{2,1,0:T(8,128)(2,1)S(1)}, bf16[1,256,256]{2,1,0:T(8,128)(2,1)S(1)}, u32[]{:S(2)}, u32[]{:S(2)}) %collective-permute-start.9) | collective-permute-done | bytes 131104 | tf_op jit(solution)/shard_map/ppermute | solution.py:229
  70.3 1.9 %shard_map.73 = f32[1,256,256]{2,1,0:T(8,128)} custom-call(f32[256,256]{1,0:T(8,128)S(1)} %get-tuple-element.36.moment_ref, bf16[1,256,256]{2,1,0:T(8,128)(2,1)S(1)} %collective-permute-done.9.back_ref, f32[16,64]{1,0:T(8,128)S(1)} %cosine_multiply_fusion.basis_ref), custom_call_target="tpu_custom_call" | custom-call | flops 20000000000 | tf_op jit(solution)/shard_map/pallas_call | solution.py:208
  72.2 4.4 %all-to-all-done.every_ref = bf16[16,32,128]{2,1,0:T(8,128)(2,1)S(1)} async-done(((bf16[16,32,128]{2,1,0:T(8,128)(2,1)}), bf16[16,32,128]{2,1,0:T(8,128)(2,1)S(1)}, u32[]{:S(2)}, u32[]{:S(2)}) %all-to-all-start) | async-done | bytes 131104 | tf_op jit(solution)/shard_map/all_to_all | solution.py:266
  76.6 1.4 %shard_map.75 = f32[256,256]{1,0:T(8,128)} custom-call(bf16[16,32,128]{2,1,0:T(8,128)(2,1)S(1)} %all-to-all-done.every_ref, f32[16,64]{1,0:T(8,128)S(1)} %cosine_multiply_fusion.basis_ref), custom_call_target="tpu_custom_call" | custom-call | tf_op jit(solution)/shard_map/pallas_call | solution.py:208
  (7 shorter events, 0.2 us)
Async XLA Ops:
  3.3 4.6 %collective-permute-start = (bf16[8,256,256]{2,1,0:T(8,128)(2,1)S(1)}, bf16[8,256,256]{2,1,0:T(8,128)(2,1)S(1)}, u32[]{:S(2)}, u32[]{:S(2)}) collective-permute-start(bf16[8,256,256]{2,1,0:T(8,128)(2,1)S(1)} %get-tuple-element.23), channel_id=1, source_target_pairs={{0,1},{1,0},{2,3},{3,2},{4,5},{5,4},{6,7},{7,6},{8,9},{9,8},{10,11... | collective-permute-start | bytes 3145736 | tf_op jit(solution)/shard_map/ppermute | solution.py:229
  8.0 12.6 %collective-permute-start.3 = (bf16[4,256,256]{2,1,0:T(8,128)(2,1)S(1)}, bf16[4,256,256]{2,1,0:T(8,128)(2,1)S(1)}, u32[]{:S(2)}, u32[]{:S(2)}) collective-permute-start(bf16[4,256,256]{2,1,0:T(8,128)(2,1)S(1)} %shard_map.61), channel_id=1, source_target_pairs={{0,2},{1,7},{2,0},{3,5},{4,6},{5,3},{6,4},{7,1},{8,10},{9,15},{10,... | collective-permute-start | bytes 1572872 | tf_op jit(solution)/shard_map/ppermute | solution.py:229
  11.2 9.4 %collective-permute-start.1 = (bf16[8,256,256]{2,1,0:T(8,128)(2,1)S(1)}, bf16[8,256,256]{2,1,0:T(8,128)(2,1)S(1)}, u32[]{:S(2)}, u32[]{:S(2)}) collective-permute-start(bf16[8,256,256]{2,1,0:T(8,128)(2,1)S(1)} %shard_map.62), channel_id=1, source_target_pairs={{0,1},{1,0},{2,3},{3,2},{4,5},{5,4},{6,7},{7,6},{8,9},{9,8},{10,11... | collective-permute-start | bytes 3145736 | tf_op jit(solution)/shard_map/ppermute | solution.py:229
  18.2 8.9 %copy-start.1 = (s32[16]{0:T(128)S(1)}, s32[16]{0:T(128)}, u32[]{:S(2)}) copy-start(s32[16]{0:T(128)} %param.7) | copy-start | bytes 196
  18.2 18.5 %collective-permute-start.2 = (bf16[4,256,256]{2,1,0:T(8,128)(2,1)S(1)}, bf16[4,256,256]{2,1,0:T(8,128)(2,1)S(1)}, u32[]{:S(2)}, u32[]{:S(2)}) collective-permute-start(bf16[4,256,256]{2,1,0:T(8,128)(2,1)S(1)} %shard_map.63), channel_id=1, source_target_pairs={{0,2},{1,7},{2,0},{3,5},{4,6},{5,3},{6,4},{7,1},{8,10},{9,15},{10,... | collective-permute-start | bytes 1572872 | tf_op jit(solution)/shard_map/ppermute | solution.py:229
  20.8 10.1 %collective-permute-start.4 = (bf16[1,256,256]{2,1,0:T(8,128)(2,1)S(1)}, bf16[1,256,256]{2,1,0:T(8,128)(2,1)S(1)}, u32[]{:S(2)}, u32[]{:S(2)}) collective-permute-start(bf16[1,256,256]{2,1,0:T(8,128)(2,1)S(1)} %get-tuple-element.28), channel_id=1, source_target_pairs={{0,6},{1,3},{2,4},{3,1},{4,2},{5,7},{6,0},{7,5},{8,14},{9,11},{10,... | collective-permute-start | bytes 393224 | tf_op jit(solution)/shard_map/ppermute | solution.py:229
  27.1 12.6 %collective-permute-start.7 = (bf16[1,256,256]{2,1,0:T(8,128)(2,1)S(1)}, bf16[1,256,256]{2,1,0:T(8,128)(2,1)S(1)}, u32[]{:S(2)}, u32[]{:S(2)}) collective-permute-start(bf16[1,256,256]{2,1,0:T(8,128)(2,1)S(1)} %get-tuple-element.34), channel_id=1, source_target_pairs={{0,6},{1,3},{2,4},{3,1},{4,2},{5,7},{6,0},{7,5},{8,14},{9,11},{10,... | collective-permute-start | bytes 393224 | tf_op jit(solution)/shard_map/ppermute | solution.py:229
  30.9 14.4 %collective-permute-start.5 = (bf16[1,256,256]{2,1,0:T(8,128)(2,1)S(1)}, bf16[1,256,256]{2,1,0:T(8,128)(2,1)S(1)}, u32[]{:S(2)}, u32[]{:S(2)}) collective-permute-start(bf16[1,256,256]{2,1,0:T(8,128)(2,1)S(1)} %shard_map.66), channel_id=1, source_target_pairs={{0,8},{1,25},{2,10},{3,27},{4,12},{5,29},{6,14},{7,31},{8,0},{9,17... | collective-permute-start | bytes 393224 | tf_op jit(solution)/shard_map/ppermute | solution.py:229
  36.8 9.5 %collective-permute-start.6 = (bf16[2,256,256]{2,1,0:T(8,128)(2,1)S(1)}, bf16[2,256,256]{2,1,0:T(8,128)(2,1)S(1)}, u32[]{:S(2)}, u32[]{:S(2)}) collective-permute-start(bf16[2,256,256]{2,1,0:T(8,128)(2,1)S(1)} %get-tuple-element.31), channel_id=1, source_target_pairs={{0,6},{1,3},{2,4},{3,1},{4,2},{5,7},{6,0},{7,5},{8,14},{9,11},{10,... | collective-permute-start | bytes 786440 | tf_op jit(solution)/shard_map/ppermute | solution.py:229
  39.7 18.5 %collective-permute-start.8 = (bf16[1,256,256]{2,1,0:T(8,128)(2,1)S(1)}, bf16[1,256,256]{2,1,0:T(8,128)(2,1)S(1)}, u32[]{:S(2)}, u32[]{:S(2)}) collective-permute-start(bf16[1,256,256]{2,1,0:T(8,128)(2,1)S(1)} %shard_map.70), channel_id=1, source_target_pairs={{0,8},{1,25},{2,10},{3,27},{4,12},{5,29},{6,14},{7,31},{8,0},{9,17... | collective-permute-start | bytes 393224 | tf_op jit(solution)/shard_map/ppermute | solution.py:229
  47.0 11.3 %copy-start = (f32[1,256,256]{2,1,0:T(8,128)S(1)}, f32[1,256,256]{2,1,0:T(8,128)}, u32[]{:S(2)}) copy-start(f32[1,256,256]{2,1,0:T(8,128)} %momentum_ref.1) | copy-start | bytes 786436
  47.0 11.9 %collective-permute-start.10 = (f32[32,128]{1,0:T(8,128)S(1)}, f32[32,128]{1,0:T(8,128)S(1)}, u32[]{:S(2)}, u32[]{:S(2)}) collective-permute-start(f32[32,128]{1,0:T(8,128)S(1)} %get-tuple-element.37), channel_id=1, source_target_pairs={{0,24},{1,9},{2,26},{3,11},{4,28},{5,13},{6,30},{7,15},{8,16},{9,1... | collective-permute-start | bytes 49160 | tf_op jit(solution)/shard_map/ppermute | solution.py:229
  56.3 13.9 %collective-permute-start.9 = (bf16[1,256,256]{2,1,0:T(8,128)(2,1)S(1)}, bf16[1,256,256]{2,1,0:T(8,128)(2,1)S(1)}, u32[]{:S(2)}, u32[]{:S(2)}) collective-permute-start(bf16[1,256,256]{2,1,0:T(8,128)(2,1)S(1)} %shard_map.72), channel_id=1, source_target_pairs={{0,24},{1,9},{2,26},{3,11},{4,28},{5,13},{6,30},{7,15},{8,16},{9,1... | collective-permute-start | bytes 393224 | tf_op jit(solution)/shard_map/ppermute | solution.py:229
  59.7 16.9 %all-to-all-start = ((bf16[16,32,128]{2,1,0:T(8,128)(2,1)}), bf16[16,32,128]{2,1,0:T(8,128)(2,1)S(1)}, u32[]{:S(2)}, u32[]{:S(2)}) async-start(bf16[16,32,128]{2,1,0:T(8,128)(2,1)} %shard_map.74), calls=%async_computation | async-start | bytes 262144 | tf_op jit(solution)/shard_map/all_to_all | solution.py:266

commit v5 on v4

--- a/solution.py
+++ b/solution.py
@@ -35,8 +35,8 @@
 
 
 CORE = pairs(lambda zh, x, c: (zh, x, 1 - c))
-X1 = pairs(lambda zh, x, c: (zh, x ^ MASKS[c][2], c))
-X2 = pairs(lambda zh, x, c: (zh, x ^ MASKS[c][1], c))
+X1 = pairs(lambda zh, x, c: (zh, x ^ MASKS[1 - c][2], c))
+X2 = pairs(lambda zh, x, c: (zh, x ^ MASKS[1 - c][1], c))
 Z1 = pairs(lambda zh, x, c: (zh ^ MASKS[c][2], x, c))
 Z2 = pairs(lambda zh, x, c: (zh ^ MASKS[c][1], x, c))
 
@@ -51,7 +51,7 @@
     zh = me // (2 * RING)
     if flip:
         c = 1 - c
-    mx = jnp.where(c == 0, MASKS[0][p], MASKS[1][p])
+    mx = jnp.where(c == 0, MASKS[1][p], MASKS[0][p])
     mz = jnp.where(c == 0, MASKS[0][q], MASKS[1][q])
     return pl.multiple_of((((zh ^ mz) * RING + (x ^ mx)) * 2 + c) * UNIT, UNIT)
 
@@ -156,52 +156,78 @@
     return jnp.dot(a, b, precision=HIGH, preferred_element_type=F32)
 
 
-def block_basis(basis, blocks):
+def turned(a, b):
+    return lax.dot_general(a, b, (((1,), (1,)), ((), ())), precision=HIGH, preferred_element_type=F32)
+
+
+def split(a):
+    high = a.astype(BF16)
+    return high, (a - high.astype(F32)).astype(BF16)
+
+
+def pack(coeffs):
+    half = coeffs.shape[0] // 2
+    return jnp.concatenate([coeffs[:half], coeffs[half:]], axis=1)
+
+
+def unpack(packed):
+    half = packed.shape[1] // 2
+    return jnp.concatenate([packed[:, :half], packed[:, half:]], axis=0)
+
+
+def basis_kernel(basis_ref, momentum_ref, wide_ref, tall_ref, rows_ref, right_ref, left_ref, coeffs_ref):
+    basis = basis_ref[...]
     k, n = basis.shape
+    blocks = wide_ref.shape[0] // k
     wide = jnp.concatenate([jnp.concatenate([basis] * blocks, axis=1)] * blocks, axis=0)
     row = lax.broadcasted_iota(jnp.int32, wide.shape, 0) // k
     col = lax.broadcasted_iota(jnp.int32, wide.shape, 1) // n
-    return jnp.where(row == col, wide, 0.0)
-
-
-def coeffs_of(basis, moment):
-    wide = block_basis(basis, moment.shape[0] // SPAN)
-    coeffs = dot(dot(wide, moment), wide.T)
-    half = coeffs.shape[0] // 2
-    return coeffs, jnp.concatenate([coeffs[:half], coeffs[half:]], axis=1)
-
-
-def late_kernel(near_ref, away_ref, back_ref, basis_ref, near_out_ref, coeffs_ref):
+    wide = jnp.where(row == col, wide, 0.0)
+    tall = wide.T
+    wide_ref[...] = wide
+    tall_ref[...] = tall
+    high, low = split(wide)
+    rows_ref[...] = jnp.concatenate([high, low], axis=0)
+    right_ref[...] = jnp.concatenate([high, high, low], axis=0)
+    high, low = split(tall)
+    left_ref[...] = jnp.concatenate([high, low, high], axis=1)
+    coeffs_ref[...] = pack(turned(dot(wide, 0.9 * momentum_ref[0]), wide).T)
+
+
+def along_rows(rows, block):
+    both = jnp.dot(rows, block, preferred_element_type=F32)
+    half = both.shape[0] // 2
+    return both[:half] + both[half:]
+
+
+def late_kernel(near_ref, away_ref, back_ref, wide_ref, rows_ref, near_out_ref, coeffs_ref):
     near_out_ref[0] = (near_ref[0].astype(F32) + back_ref[0].astype(F32)).astype(BF16)
     away = (away_ref[0].astype(F32) + back_ref[1].astype(F32)).astype(BF16)
-    coeffs_ref[...] = coeffs_of(basis_ref[...], away.astype(F32).T)[1]
-
-
-def near_kernel(near_ref, back_ref, momentum_ref, basis_ref, moment_ref, coeffs_ref):
-    moment = 0.9 * momentum_ref[0] + (near_ref[0].astype(F32) + back_ref[0].astype(F32)).T
-    moment_ref[...] = moment
-    coeffs_ref[...] = coeffs_of(basis_ref[...], moment)[1]
-
-
-def sent_kernel(a_ref, b_ref, sent_ref):
-    sent = (a_ref[...] + b_ref[...]).astype(BF16)
+    coeffs_ref[...] = pack(turned(along_rows(rows_ref[...], away), wide_ref[...]))
+
+
+def sent_kernel(near_ref, back_ref, own_ref, other_ref, wide_ref, rows_ref, sent_ref):
+    rows = rows_ref[...]
+    kept = along_rows(rows, near_ref[0]) + along_rows(rows, back_ref[0])
+    sent = (pack(turned(kept, wide_ref[...])) + own_ref[...] + other_ref[...]).astype(BF16)
     for r in range(sent_ref.shape[0]):
         sent_ref[r] = sent
 
 
-def new_kernel(moment_ref, back_ref, basis_ref, out_ref):
-    moment = moment_ref[...] + back_ref[0].astype(F32).T
-    basis = basis_ref[...]
-    wide = block_basis(basis, moment.shape[1] // SPAN)
-    out_ref[0] = moment - dot(wide.T, dot(coeffs_of(basis, moment)[0], wide))
-
-
-def update_kernel(every_ref, basis_ref, update_ref):
-    total = jnp.sum(every_ref[...].astype(F32), axis=0)
-    n = total.shape[1] // 2
-    mean = jnp.concatenate([total[:, :n], total[:, n:]], axis=0) * (4.0 / every_ref.shape[0])
-    wide = block_basis(basis_ref[...], update_ref.shape[1] // SPAN)
-    update_ref[...] = dot(wide.T, dot(mean, wide))
+def new_kernel(momentum_ref, near_ref, r2_ref, r1_ref, wide_ref, tall_ref, out_ref):
+    grad = near_ref[0].astype(F32) + r2_ref[0].astype(F32) + r1_ref[0].astype(F32)
+    moment = 0.9 * momentum_ref[0] + grad.T
+    wide, tall = wide_ref[...], tall_ref[...]
+    out_ref[0] = moment - dot(tall, dot(dot(dot(wide, moment), tall), wide))
+
+
+def update_kernel(every_ref, right_ref, left_ref, update_ref):
+    total = jnp.sum(every_ref[...].astype(F32), axis=0) * (4.0 / every_ref.shape[0])
+    high, low = split(unpack(total).T)
+    mean = jnp.concatenate([high, low, high], axis=1)
+    high, low = split(jnp.dot(mean, right_ref[...], preferred_element_type=F32))
+    mean = jnp.concatenate([high, high, low], axis=0)
+    update_ref[...] = jnp.dot(left_ref[...], mean, preferred_element_type=F32)
 
 
 def on_vmem(kernel, out_shape, *args, cost=None):
@@ -233,7 +259,24 @@
 
     got, held, left = first_product(places(True, EARLY + LATE), me, tokens, grad_hidden)
     got = swap(got, CORE)
-    own = product(places(False, EARLY + LATE), me, left, held)
+    basis = kept_basis(kept)
+    kw = cols // SPAN * KEEP
+    packed = pltpu.VMEM((kw // 2, kw * 2), F32)
+    unit = pltpu.VMEM((1, cols, rows), BF16)
+    wide, tall, in_rows, on_right, on_left, own_coeffs = on_vmem(
+        basis_kernel,
+        (
+            pltpu.VMEM((kw, cols), F32),
+            pltpu.VMEM((cols, kw), F32),
+            pltpu.VMEM((2 * kw, cols), BF16),
+            pltpu.VMEM((3 * kw, cols), BF16),
+            pltpu.VMEM((cols, 3 * kw), BF16),
+            packed,
+        ),
+        basis,
+        momentum,
+    )
+    own = product(places(False, EARLY + LATE), me, after(left, own_coeffs), held)
     (early_away,) = add([(own, 0), (got, 0)], (4,))
     early_back = swap(early_away, X1)
     left = after(left, early_away)
@@ -253,19 +296,16 @@
     r2 = swap(a2, Z1)
     (away,) = add([(near, 1), (r3, 0)], (1,), LONG)
 
-    basis = kept_basis(kept)
-    kw = cols // SPAN * KEEP
-    packed = pltpu.VMEM((kw // 2, kw * 2), F32)
-    unit = pltpu.VMEM(away.shape, BF16)
-    b0, coeffs1 = on_vmem(late_kernel, (unit, packed), near, away, late_back, basis)
-    (away,) = add([(away, 0), (after(late_back, coeffs1), 1)], (1,), LONG)
-    coeffs1 = swap(coeffs1, Z2)
-    moment, coeffs0 = on_vmem(near_kernel, (pltpu.VMEM((rows, cols), F32), packed), b0, r2, momentum, basis)
+    b0, coeffs = on_vmem(late_kernel, (unit, packed), near, away, late_back, wide, in_rows)
+    (away,) = add([(away, 0), (after(late_back, coeffs), 1)], (1,), LONG)
+    coeffs = swap(coeffs, Z2)
     r1 = swap(away, Z2)
-    sent = on_vmem(sent_kernel, pltpu.VMEM((n_dp, kw // 2, kw * 2), BF16), coeffs0, coeffs1, cost=LONG)
+    sent_shape = pltpu.VMEM((n_dp, kw // 2, kw * 2), BF16)
+    sent = on_vmem(sent_kernel, sent_shape, b0, r2, own_coeffs, coeffs, wide, in_rows, cost=LONG)
     every = lax.all_to_all(sent, "dp", 0, 0, tiled=True)
-    new_momentum = on_vmem(new_kernel, jax.ShapeDtypeStruct((1, rows, cols), F32), moment, r1, basis, cost=LONG)
-    update = on_vmem(update_kernel, jax.ShapeDtypeStruct((rows, cols), F32), every, basis)
+    new_shape = jax.ShapeDtypeStruct((1, rows, cols), F32)
+    new_momentum = on_vmem(new_kernel, new_shape, momentum, b0, r2, r1, wide, tall, cost=LONG)
+    update = on_vmem(update_kernel, jax.ShapeDtypeStruct((rows, cols), F32), every, on_right, on_left)
     return new_momentum, update
 
 

time: 78.4 us -> 76.6 us (0.977)
  starting transfers between devices: 54.6 us -> 48.2 us
  waiting for transfers between devices: 12 us -> 15.8 us
    ppermute x11, waiting for transfers between devices: 7.6 us -> 12.9 us  [swap(): return lax.ppermute(a, 'fsdp', perm)]
    ppermute x11, starting transfers between devices: 46.7 us -> 42.7 us  [swap(): return lax.ppermute(a, 'fsdp', perm)]
    all_to_all x1, starting transfers between devices: 7.95 us -> 5.47 us  [on_device(): every = lax.all_to_all(sent, 'dp', 0, 0, tiled=True)]
    all_to_all x1, waiting for transfers between devices: 4.41 us -> 2.95 us  [on_device(): every = lax.all_to_all(sent, 'dp', 0, 0, tiled=True)]
  transfers between devices with their start and end apart: 12 -> 12, of which waited for: 5 -> 7; matrix products, arithmetic and copies ran while one was open for 0% -> 0% of each run, Pallas kernels for 8% -> 8%
where the time goes in v5:
time: 76.6 us; the launch traced here: 75.4 us
  starting transfers between devices  48.2 us (63%)
  waiting for transfers between devices  15.8 us (21%)
  Pallas kernels  10.4 us (14%)
  between operations  0.9 us (1%)
    ppermute x11, starting transfers between devices, swap(): return lax.ppermute(a, 'fsdp', perm)  42.7 us
    ppermute x11, waiting for transfers between devices, swap(): return lax.ppermute(a, 'fsdp', perm)  12.9 us
    all_to_all x1, starting transfers between devices, on_device(): every = lax.all_to_all(sent, 'dp', 0, 0, tiled=True)  5.47 us
    pallas_call x5, Pallas kernels, on_vmem(): pl.pallas_call(kernel, out_shape=out_shape, in_specs=[IN_VMEM] * len(args...  5.41 us
    all_to_all x1, waiting for transfers between devices, on_device(): every = lax.all_to_all(sent, 'dp', 0, 0, tiled=True)  2.95 us
    pallas_call x1, Pallas kernels, first_product(): pl.pallas_call(functools.partial(first_kernel, places), out_shape=(pltpu....  2.75 us
  transfers between devices with their start and end apart: 12, of which 7 were waited for; matrix products, arithmetic and copies ran while one was open for 0% of the time, Pallas kernels for 8%

profile of v5, /device:TPU:6, one launch (start us, length us, event | category | flops | bytes accessed | tf_op | source)
XLA Modules:
  0.0 75.4 jit_solution(3324453957143499076)
XLA Ops:
  0.6 0.0 copy-start.1
  0.6 0.0 copy-start
  0.7 2.7 %shard_map.59 = (bf16[8,256,256]{2,1,0:T(8,128)(2,1)S(1)}, bf16[256,8192]{1,0:T(8,128)(2,1)S(1)}, bf16[256,256]{1,0:T(8,128)(2,1)S(1)}) custom-call(s32[1]{0:T(128)} %bitcast.me_ref, bf16[256,8192]{1,0:T(8,128)(2,1)} %tokens_ref.1, bf16[256,256]{1,0:T(8,128)(2,1)} %hidden_ref.1), custom_call_target="tpu_custom_call" | custom-call | tf_op jit(solution)/shard_map/pallas_call | solution.py:88
  3.4 1.9 %collective-permute-start = (bf16[8,256,256]{2,1,0:T(8,128)(2,1)S(1)}, bf16[8,256,256]{2,1,0:T(8,128)(2,1)S(1)}, u32[]{:S(2)}, u32[]{:S(2)}) collective-permute-start(bf16[8,256,256]{2,1,0:T(8,128)(2,1)S(1)} %get-tuple-element.30), channel_id=1, source_target_pairs={{0,1},{1,0},{2,3},{3,2},{4,5},{5,4},{6,7},{7,6},{8,9},{9,8},{10,11... | collective-permute-start | bytes 3145736 | tf_op jit(solution)/shard_map/ppermute | solution.py:255
  5.3 0.0 copy-done.1
  5.4 0.1 cosine_multiply_fusion.basis_ref
  5.5 0.0 copy-done
  5.5 0.6 shard_map.60
  6.2 0.5 shard_map.61.refs_0_
  6.7 1.3 %collective-permute-done.refs_1_ = bf16[8,256,256]{2,1,0:T(8,128)(2,1)S(1)} collective-permute-done((bf16[8,256,256]{2,1,0:T(8,128)(2,1)S(1)}, bf16[8,256,256]{2,1,0:T(8,128)(2,1)S(1)}, u32[]{:S(2)}, u32[]{:S(2)}) %collective-permute-start) | collective-permute-done | bytes 1048608 | tf_op jit(solution)/shard_map/ppermute | solution.py:255
  8.0 0.1 shard_map.62
  8.1 7.8 %collective-permute-start.3 = (bf16[4,256,256]{2,1,0:T(8,128)(2,1)S(1)}, bf16[4,256,256]{2,1,0:T(8,128)(2,1)S(1)}, u32[]{:S(2)}, u32[]{:S(2)}) collective-permute-start(bf16[4,256,256]{2,1,0:T(8,128)(2,1)S(1)} %shard_map.62), channel_id=1, source_target_pairs={{0,6},{1,3},{2,4},{3,1},{4,2},{5,7},{6,0},{7,5},{8,14},{9,11},{10,... | collective-permute-start | bytes 1572872 | tf_op jit(solution)/shard_map/ppermute | solution.py:255
  15.9 0.5 shard_map.63
  16.3 0.1 shard_map.64
  16.5 1.9 %collective-permute-start.2 = (bf16[4,256,256]{2,1,0:T(8,128)(2,1)S(1)}, bf16[4,256,256]{2,1,0:T(8,128)(2,1)S(1)}, u32[]{:S(2)}, u32[]{:S(2)}) collective-permute-start(bf16[4,256,256]{2,1,0:T(8,128)(2,1)S(1)} %shard_map.64), channel_id=1, source_target_pairs={{0,6},{1,3},{2,4},{3,1},{4,2},{5,7},{6,0},{7,5},{8,14},{9,11},{10,... | collective-permute-start | bytes 1572872 | tf_op jit(solution)/shard_map/ppermute | solution.py:255
  18.4 1.9 %collective-permute-start.1 = (bf16[8,256,256]{2,1,0:T(8,128)(2,1)S(1)}, bf16[8,256,256]{2,1,0:T(8,128)(2,1)S(1)}, u32[]{:S(2)}, u32[]{:S(2)}) collective-permute-start(bf16[8,256,256]{2,1,0:T(8,128)(2,1)S(1)} %shard_map.63), channel_id=1, source_target_pairs={{0,1},{1,0},{2,3},{3,2},{4,5},{5,4},{6,7},{7,6},{8,9},{9,8},{10,11... | collective-permute-start | bytes 3145736 | tf_op jit(solution)/shard_map/ppermute | solution.py:255
  20.3 0.5 shard_map.65.refs_0_
  20.8 2.2 %collective-permute-done.3.refs_2_ = bf16[4,256,256]{2,1,0:T(8,128)(2,1)S(1)} collective-permute-done((bf16[4,256,256]{2,1,0:T(8,128)(2,1)S(1)}, bf16[4,256,256]{2,1,0:T(8,128)(2,1)S(1)}, u32[]{:S(2)}, u32[]{:S(2)}) %collective-permute-start.3) | collective-permute-done | bytes 524320 | tf_op jit(solution)/shard_map/ppermute | solution.py:255
  23.0 0.0 collective-permute-done.1.refs_1_
  23.0 0.2 shard_map.66
  23.2 1.9 %collective-permute-start.4 = (bf16[1,256,256]{2,1,0:T(8,128)(2,1)S(1)}, bf16[1,256,256]{2,1,0:T(8,128)(2,1)S(1)}, u32[]{:S(2)}, u32[]{:S(2)}) collective-permute-start(bf16[1,256,256]{2,1,0:T(8,128)(2,1)S(1)} %get-tuple-element.35), channel_id=1, source_target_pairs={{0,2},{1,7},{2,0},{3,5},{4,6},{5,3},{6,4},{7,1},{8,10},{9,15},{10,... | collective-permute-start | bytes 393224 | tf_op jit(solution)/shard_map/ppermute | solution.py:255
  25.1 3.9 %collective-permute-start.7 = (bf16[1,256,256]{2,1,0:T(8,128)(2,1)S(1)}, bf16[1,256,256]{2,1,0:T(8,128)(2,1)S(1)}, u32[]{:S(2)}, u32[]{:S(2)}) collective-permute-start(bf16[1,256,256]{2,1,0:T(8,128)(2,1)S(1)} %get-tuple-element.43), channel_id=1, source_target_pairs={{0,2},{1,7},{2,0},{3,5},{4,6},{5,3},{6,4},{7,1},{8,10},{9,15},{10,... | collective-permute-start | bytes 393224 | tf_op jit(solution)/shard_map/ppermute | solution.py:255
  29.1 1.0 %collective-permute-done.4.refs_1_ = bf16[1,256,256]{2,1,0:T(8,128)(2,1)S(1)} collective-permute-done((bf16[1,256,256]{2,1,0:T(8,128)(2,1)S(1)}, bf16[1,256,256]{2,1,0:T(8,128)(2,1)S(1)}, u32[]{:S(2)}, u32[]{:S(2)}) %collective-permute-start.4) | collective-permute-done | bytes 131104 | tf_op jit(solution)/shard_map/ppermute | solution.py:255
  30.1 6.5 %collective-permute-start.5 = (bf16[1,256,256]{2,1,0:T(8,128)(2,1)S(1)}, bf16[1,256,256]{2,1,0:T(8,128)(2,1)S(1)}, u32[]{:S(2)}, u32[]{:S(2)}) collective-permute-start(bf16[1,256,256]{2,1,0:T(8,128)(2,1)S(1)} %shard_map.67), channel_id=1, source_target_pairs={{0,8},{1,25},{2,10},{3,27},{4,12},{5,29},{6,14},{7,31},{8,0},{9,17... | collective-permute-start | bytes 393224 | tf_op jit(solution)/shard_map/ppermute | solution.py:255
  36.6 0.0 collective-permute-done.2.refs_2_
  36.6 0.2 shard_map.68
  36.8 1.9 %collective-permute-start.6 = (bf16[2,256,256]{2,1,0:T(8,128)(2,1)S(1)}, bf16[2,256,256]{2,1,0:T(8,128)(2,1)S(1)}, u32[]{:S(2)}, u32[]{:S(2)}) collective-permute-start(bf16[2,256,256]{2,1,0:T(8,128)(2,1)S(1)} %get-tuple-element.38), channel_id=1, source_target_pairs={{0,2},{1,7},{2,0},{3,5},{4,6},{5,3},{6,4},{7,1},{8,10},{9,15},{10,... | collective-permute-start | bytes 786440 | tf_op jit(solution)/shard_map/ppermute | solution.py:255
  38.7 0.0 collective-permute-done.7.refs_1_
  38.8 3.3 %collective-permute-start.8 = (bf16[1,256,256]{2,1,0:T(8,128)(2,1)S(1)}, bf16[1,256,256]{2,1,0:T(8,128)(2,1)S(1)}, u32[]{:S(2)}, u32[]{:S(2)}) collective-permute-start(bf16[1,256,256]{2,1,0:T(8,128)(2,1)S(1)} %shard_map.71), channel_id=1, source_target_pairs={{0,8},{1,25},{2,10},{3,27},{4,12},{5,29},{6,14},{7,31},{8,0},{9,17... | collective-permute-start | bytes 393224 | tf_op jit(solution)/shard_map/ppermute | solution.py:255
  42.1 3.4 %collective-permute-done.5.refs_1_ = bf16[1,256,256]{2,1,0:T(8,128)(2,1)S(1)} collective-permute-done((bf16[1,256,256]{2,1,0:T(8,128)(2,1)S(1)}, bf16[1,256,256]{2,1,0:T(8,128)(2,1)S(1)}, u32[]{:S(2)}, u32[]{:S(2)}) %collective-permute-start.5) | collective-permute-done | bytes 131104 | tf_op jit(solution)/shard_map/ppermute | solution.py:255
  45.5 0.0 collective-permute-done.6.back_ref.refs_1_
  45.5 0.5 shard_map.70
  46.0 9.8 %collective-permute-start.10 = (f32[32,128]{1,0:T(8,128)S(1)}, f32[32,128]{1,0:T(8,128)S(1)}, u32[]{:S(2)}, u32[]{:S(2)}) collective-permute-start(f32[32,128]{1,0:T(8,128)S(1)} %get-tuple-element.45), channel_id=1, source_target_pairs={{0,24},{1,9},{2,26},{3,11},{4,28},{5,13},{6,30},{7,15},{8,16},{9,1... | collective-permute-start | bytes 49160 | tf_op jit(solution)/shard_map/ppermute | solution.py:255
  55.8 1.9 %collective-permute-start.9 = (bf16[1,256,256]{2,1,0:T(8,128)(2,1)S(1)}, bf16[1,256,256]{2,1,0:T(8,128)(2,1)S(1)}, u32[]{:S(2)}, u32[]{:S(2)}) collective-permute-start(bf16[1,256,256]{2,1,0:T(8,128)(2,1)S(1)} %shard_map.72), channel_id=1, source_target_pairs={{0,24},{1,9},{2,26},{3,11},{4,28},{5,13},{6,30},{7,15},{8,16},{9,1... | collective-permute-start | bytes 393224 | tf_op jit(solution)/shard_map/ppermute | solution.py:255
  57.7 0.0 collective-permute-done.8.r2_ref.back_ref
  57.7 0.8 %collective-permute-done.10.other_ref = f32[32,128]{1,0:T(8,128)S(1)} collective-permute-done((f32[32,128]{1,0:T(8,128)S(1)}, f32[32,128]{1,0:T(8,128)S(1)}, u32[]{:S(2)}, u32[]{:S(2)}) %collective-permute-start.10) | collective-permute-done | bytes 16416 | tf_op jit(solution)/shard_map/ppermute | solution.py:255
  58.5 1.1 %shard_map.74 = bf16[16,32,128]{2,1,0:T(8,128)(2,1)} custom-call(bf16[1,256,256]{2,1,0:T(8,128)(2,1)S(1)} %get-tuple-element.41.near_ref, bf16[1,256,256]{2,1,0:T(8,128)(2,1)S(1)} %collective-permute-done.8.r2_ref.back_ref, f32[32,128]{1,0:T(8,128)S(1)} %get-tuple-element.27.own_ref, f32[32,128]{1,0:T(8,128)S(1)} %collective-permute-done.10.other_ref, ...), custom_call_target="tpu_custom_call" | custom-call | flops 20000000000 | tf_op jit(solution)/shard_map/pallas_call | solution.py:234
  59.7 5.5 %all-to-all-start = ((bf16[16,32,128]{2,1,0:T(8,128)(2,1)}), bf16[16,32,128]{2,1,0:T(8,128)(2,1)S(1)}, u32[]{:S(2)}, u32[]{:S(2)}) async-start(bf16[16,32,128]{2,1,0:T(8,128)(2,1)} %shard_map.74), calls=%async_computation | async-start | bytes 262144 | tf_op jit(solution)/shard_map/all_to_all | solution.py:305
  65.2 4.2 %collective-permute-done.9.r1_ref = bf16[1,256,256]{2,1,0:T(8,128)(2,1)S(1)} collective-permute-done((bf16[1,256,256]{2,1,0:T(8,128)(2,1)S(1)}, bf16[1,256,256]{2,1,0:T(8,128)(2,1)S(1)}, u32[]{:S(2)}, u32[]{:S(2)}) %collective-permute-start.9) | collective-permute-done | bytes 131104 | tf_op jit(solution)/shard_map/ppermute | solution.py:255
  69.3 1.9 %shard_map.73 = f32[1,256,256]{2,1,0:T(8,128)} custom-call(f32[1,256,256]{2,1,0:T(8,128)S(1)} %copy-done, bf16[1,256,256]{2,1,0:T(8,128)(2,1)S(1)} %get-tuple-element.41.near_ref, bf16[1,256,256]{2,1,0:T(8,128)(2,1)S(1)} %collective-permute-done.8.r2_ref.back_ref, bf16[1,256,256]{2,1,0:T(8,128)(2,1)S(1)} %collective-permute-done.9.r1_ref, ...), custom_call_target="tpu_custom_call" | custom-call | flops 20000000000 | tf_op jit(solution)/shard_map/pallas_call | solution.py:234
  71.2 2.9 %all-to-all-done.every_ref = bf16[16,32,128]{2,1,0:T(8,128)(2,1)S(1)} async-done(((bf16[16,32,128]{2,1,0:T(8,128)(2,1)}), bf16[16,32,128]{2,1,0:T(8,128)(2,1)S(1)}, u32[]{:S(2)}, u32[]{:S(2)}) %all-to-all-start) | async-done | bytes 131104 | tf_op jit(solution)/shard_map/all_to_all | solution.py:305
  74.2 1.2 %shard_map.75 = f32[256,256]{1,0:T(8,128)} custom-call(bf16[16,32,128]{2,1,0:T(8,128)(2,1)S(1)} %all-to-all-done.every_ref, bf16[192,256]{1,0:T(8,128)(2,1)S(1)} %get-tuple-element.48.right_ref, bf16[256,192]{1,0:T(8,128)(2,1)S(1)} %get-tuple-element.49.left_ref), custom_call_target="tpu_custom_call" | custom-call | tf_op jit(solution)/shard_map/pallas_call | solution.py:234
  (7 shorter events, 0.1 us)
Async XLA Ops:
  0.6 4.7 %copy-start.1 = (s32[16]{0:T(128)S(1)}, s32[16]{0:T(128)}, u32[]{:S(2)}) copy-start(s32[16]{0:T(128)} %param.7) | copy-start | bytes 196
  0.6 4.9 %copy-start = (f32[1,256,256]{2,1,0:T(8,128)S(1)}, f32[1,256,256]{2,1,0:T(8,128)}, u32[]{:S(2)}) copy-start(f32[1,256,256]{2,1,0:T(8,128)} %momentum_ref.3) | copy-start | bytes 786436
  3.4 4.6 %collective-permute-start = (bf16[8,256,256]{2,1,0:T(8,128)(2,1)S(1)}, bf16[8,256,256]{2,1,0:T(8,128)(2,1)S(1)}, u32[]{:S(2)}, u32[]{:S(2)}) collective-permute-start(bf16[8,256,256]{2,1,0:T(8,128)(2,1)S(1)} %get-tuple-element.30), channel_id=1, source_target_pairs={{0,1},{1,0},{2,3},{3,2},{4,5},{5,4},{6,7},{7,6},{8,9},{9,8},{10,11... | collective-permute-start | bytes 3145736 | tf_op jit(solution)/shard_map/ppermute | solution.py:255
  8.1 14.9 %collective-permute-start.3 = (bf16[4,256,256]{2,1,0:T(8,128)(2,1)S(1)}, bf16[4,256,256]{2,1,0:T(8,128)(2,1)S(1)}, u32[]{:S(2)}, u32[]{:S(2)}) collective-permute-start(bf16[4,256,256]{2,1,0:T(8,128)(2,1)S(1)} %shard_map.62), channel_id=1, source_target_pairs={{0,6},{1,3},{2,4},{3,1},{4,2},{5,7},{6,0},{7,5},{8,14},{9,11},{10,... | collective-permute-start | bytes 1572872 | tf_op jit(solution)/shard_map/ppermute | solution.py:255
  16.5 20.1 %collective-permute-start.2 = (bf16[4,256,256]{2,1,0:T(8,128)(2,1)S(1)}, bf16[4,256,256]{2,1,0:T(8,128)(2,1)S(1)}, u32[]{:S(2)}, u32[]{:S(2)}) collective-permute-start(bf16[4,256,256]{2,1,0:T(8,128)(2,1)S(1)} %shard_map.64), channel_id=1, source_target_pairs={{0,6},{1,3},{2,4},{3,1},{4,2},{5,7},{6,0},{7,5},{8,14},{9,11},{10,... | collective-permute-start | bytes 1572872 | tf_op jit(solution)/shard_map/ppermute | solution.py:255
  18.4 4.6 %collective-permute-start.1 = (bf16[8,256,256]{2,1,0:T(8,128)(2,1)S(1)}, bf16[8,256,256]{2,1,0:T(8,128)(2,1)S(1)}, u32[]{:S(2)}, u32[]{:S(2)}) collective-permute-start(bf16[8,256,256]{2,1,0:T(8,128)(2,1)S(1)} %shard_map.63), channel_id=1, source_target_pairs={{0,1},{1,0},{2,3},{3,2},{4,5},{5,4},{6,7},{7,6},{8,9},{9,8},{10,11... | collective-permute-start | bytes 3145736 | tf_op jit(solution)/shard_map/ppermute | solution.py:255
  23.2 6.9 %collective-permute-start.4 = (bf16[1,256,256]{2,1,0:T(8,128)(2,1)S(1)}, bf16[1,256,256]{2,1,0:T(8,128)(2,1)S(1)}, u32[]{:S(2)}, u32[]{:S(2)}) collective-permute-start(bf16[1,256,256]{2,1,0:T(8,128)(2,1)S(1)} %get-tuple-element.35), channel_id=1, source_target_pairs={{0,2},{1,7},{2,0},{3,5},{4,6},{5,3},{6,4},{7,1},{8,10},{9,15},{10,... | collective-permute-start | bytes 393224 | tf_op jit(solution)/shard_map/ppermute | solution.py:255
  25.1 13.6 %collective-permute-start.7 = (bf16[1,256,256]{2,1,0:T(8,128)(2,1)S(1)}, bf16[1,256,256]{2,1,0:T(8,128)(2,1)S(1)}, u32[]{:S(2)}, u32[]{:S(2)}) collective-permute-start(bf16[1,256,256]{2,1,0:T(8,128)(2,1)S(1)} %get-tuple-element.43), channel_id=1, source_target_pairs={{0,2},{1,7},{2,0},{3,5},{4,6},{5,3},{6,4},{7,1},{8,10},{9,15},{10,... | collective-permute-start | bytes 393224 | tf_op jit(solution)/shard_map/ppermute | solution.py:255
  30.1 15.3 %collective-permute-start.5 = (bf16[1,256,256]{2,1,0:T(8,128)(2,1)S(1)}, bf16[1,256,256]{2,1,0:T(8,128)(2,1)S(1)}, u32[]{:S(2)}, u32[]{:S(2)}) collective-permute-start(bf16[1,256,256]{2,1,0:T(8,128)(2,1)S(1)} %shard_map.67), channel_id=1, source_target_pairs={{0,8},{1,25},{2,10},{3,27},{4,12},{5,29},{6,14},{7,31},{8,0},{9,17... | collective-permute-start | bytes 393224 | tf_op jit(solution)/shard_map/ppermute | solution.py:255
  36.8 8.7 %collective-permute-start.6 = (bf16[2,256,256]{2,1,0:T(8,128)(2,1)S(1)}, bf16[2,256,256]{2,1,0:T(8,128)(2,1)S(1)}, u32[]{:S(2)}, u32[]{:S(2)}) collective-permute-start(bf16[2,256,256]{2,1,0:T(8,128)(2,1)S(1)} %get-tuple-element.38), channel_id=1, source_target_pairs={{0,2},{1,7},{2,0},{3,5},{4,6},{5,3},{6,4},{7,1},{8,10},{9,15},{10,... | collective-permute-start | bytes 786440 | tf_op jit(solution)/shard_map/ppermute | solution.py:255
  38.8 18.9 %collective-permute-start.8 = (bf16[1,256,256]{2,1,0:T(8,128)(2,1)S(1)}, bf16[1,256,256]{2,1,0:T(8,128)(2,1)S(1)}, u32[]{:S(2)}, u32[]{:S(2)}) collective-permute-start(bf16[1,256,256]{2,1,0:T(8,128)(2,1)S(1)} %shard_map.71), channel_id=1, source_target_pairs={{0,8},{1,25},{2,10},{3,27},{4,12},{5,29},{6,14},{7,31},{8,0},{9,17... | collective-permute-start | bytes 393224 | tf_op jit(solution)/shard_map/ppermute | solution.py:255
  46.0 12.6 %collective-permute-start.10 = (f32[32,128]{1,0:T(8,128)S(1)}, f32[32,128]{1,0:T(8,128)S(1)}, u32[]{:S(2)}, u32[]{:S(2)}) collective-permute-start(f32[32,128]{1,0:T(8,128)S(1)} %get-tuple-element.45), channel_id=1, source_target_pairs={{0,24},{1,9},{2,26},{3,11},{4,28},{5,13},{6,30},{7,15},{8,16},{9,1... | collective-permute-start | bytes 49160 | tf_op jit(solution)/shard_map/ppermute | solution.py:255
  55.8 13.5 %collective-permute-start.9 = (bf16[1,256,256]{2,1,0:T(8,128)(2,1)S(1)}, bf16[1,256,256]{2,1,0:T(8,128)(2,1)S(1)}, u32[]{:S(2)}, u32[]{:S(2)}) collective-permute-start(bf16[1,256,256]{2,1,0:T(8,128)(2,1)S(1)} %shard_map.72), channel_id=1, source_target_pairs={{0,24},{1,9},{2,26},{3,11},{4,28},{5,13},{6,30},{7,15},{8,16},{9,1... | collective-permute-start | bytes 393224 | tf_op jit(solution)/shard_map/ppermute | solution.py:255
  59.7 14.5 %all-to-all-start = ((bf16[16,32,128]{2,1,0:T(8,128)(2,1)}), bf16[16,32,128]{2,1,0:T(8,128)(2,1)S(1)}, u32[]{:S(2)}, u32[]{:S(2)}) async-start(bf16[16,32,128]{2,1,0:T(8,128)(2,1)} %shard_map.74), calls=%async_computation | async-start | bytes 262144 | tf_op jit(solution)/shard_map/all_to_all | solution.py:305

commit v6 on v5

--- a/solution.py
+++ b/solution.py
@@ -191,7 +191,7 @@
     right_ref[...] = jnp.concatenate([high, high, low], axis=0)
     high, low = split(tall)
     left_ref[...] = jnp.concatenate([high, low, high], axis=1)
-    coeffs_ref[...] = pack(turned(dot(wide, 0.9 * momentum_ref[0]), wide).T)
+    coeffs_ref[...] = pack(turned(dot(wide, 0.9 * momentum_ref[0]), wide))
 
 
 def along_rows(rows, block):
@@ -203,13 +203,13 @@
 def late_kernel(near_ref, away_ref, back_ref, wide_ref, rows_ref, near_out_ref, coeffs_ref):
     near_out_ref[0] = (near_ref[0].astype(F32) + back_ref[0].astype(F32)).astype(BF16)
     away = (away_ref[0].astype(F32) + back_ref[1].astype(F32)).astype(BF16)
-    coeffs_ref[...] = pack(turned(along_rows(rows_ref[...], away), wide_ref[...]))
+    coeffs_ref[...] = pack(turned(wide_ref[...], along_rows(rows_ref[...], away)))
 
 
 def sent_kernel(near_ref, back_ref, own_ref, other_ref, wide_ref, rows_ref, sent_ref):
     rows = rows_ref[...]
     kept = along_rows(rows, near_ref[0]) + along_rows(rows, back_ref[0])
-    sent = (pack(turned(kept, wide_ref[...])) + own_ref[...] + other_ref[...]).astype(BF16)
+    sent = (pack(turned(wide_ref[...], kept)) + own_ref[...] + other_ref[...]).astype(BF16)
     for r in range(sent_ref.shape[0]):
         sent_ref[r] = sent
 
@@ -223,7 +223,7 @@
 
 def update_kernel(every_ref, right_ref, left_ref, update_ref):
     total = jnp.sum(every_ref[...].astype(F32), axis=0) * (4.0 / every_ref.shape[0])
-    high, low = split(unpack(total).T)
+    high, low = split(unpack(total))
     mean = jnp.concatenate([high, low, high], axis=1)
     high, low = split(jnp.dot(mean, right_ref[...], preferred_element_type=F32))
     mean = jnp.concatenate([high, high, low], axis=0)
@@ -289,9 +289,9 @@
     back3 = swap(away3, X2)
     back2 = swap(away2, X2)
     (a3,) = add([(near3, 0), (back3, 0)], (1,))
-    r3 = swap(a3, Z1)
-    near, away = add([(own, 4), (got_rest, 4), (after(late_back, a3), 0)], (2, 2))
+    near, away = add([(own, 4), (got_rest, 4), (late_back, 0)], (2, 2))
     late_back = swap(away, X2)
+    r3 = swap(after(a3, away), Z1)
     (a2,) = add([(near2, 0), (after(back2, away), 0)], (1,))
     r2 = swap(a2, Z1)
     (away,) = add([(near, 1), (r3, 0)], (1,), LONG)

time: 76.6 us -> 76.5 us (level)
  no operation moved by 1% of the time
where the time goes in v6:
time: 76.5 us; the launch traced here: 75.2 us
  starting transfers between devices  48.2 us (63%)
  waiting for transfers between devices  15.6 us (20%)
  Pallas kernels  10.3 us (13%)
  between operations  0.89 us (1%)
    ppermute x11, starting transfers between devices, swap(): return lax.ppermute(a, 'fsdp', perm)  42.7 us
    ppermute x11, waiting for transfers between devices, swap(): return lax.ppermute(a, 'fsdp', perm)  12.9 us
    all_to_all x1, starting transfers between devices, on_device(): every = lax.all_to_all(sent, 'dp', 0, 0, tiled=True)  5.5 us
    pallas_call x5, Pallas kernels, on_vmem(): pl.pallas_call(kernel, out_shape=out_shape, in_specs=[IN_VMEM] * len(args...  5.31 us
    pallas_call x1, Pallas kernels, first_product(): pl.pallas_call(functools.partial(first_kernel, places), out_shape=(pltpu....  2.75 us
    all_to_all x1, waiting for transfers between devices, on_device(): every = lax.all_to_all(sent, 'dp', 0, 0, tiled=True)  2.75 us
  transfers between devices with their start and end apart: 12, of which 7 were waited for; matrix products, arithmetic and copies ran while one was open for 0% of the time, Pallas kernels for 8%

profile of v6, /device:TPU:6, one launch (start us, length us, event | category | flops | bytes accessed | tf_op | source)
XLA Modules:
  0.0 75.2 jit_solution(2226654662826511024)
XLA Ops:
  0.6 0.0 copy-start.1
  0.6 0.0 copy-start
  0.7 2.7 %shard_map.59 = (bf16[8,256,256]{2,1,0:T(8,128)(2,1)S(1)}, bf16[256,8192]{1,0:T(8,128)(2,1)S(1)}, bf16[256,256]{1,0:T(8,128)(2,1)S(1)}) custom-call(s32[1]{0:T(128)} %bitcast.me_ref, bf16[256,8192]{1,0:T(8,128)(2,1)} %tokens_ref.1, bf16[256,256]{1,0:T(8,128)(2,1)} %hidden_ref.1), custom_call_target="tpu_custom_call" | custom-call | tf_op jit(solution)/shard_map/pallas_call | solution.py:88
  3.4 1.9 %collective-permute-start = (bf16[8,256,256]{2,1,0:T(8,128)(2,1)S(1)}, bf16[8,256,256]{2,1,0:T(8,128)(2,1)S(1)}, u32[]{:S(2)}, u32[]{:S(2)}) collective-permute-start(bf16[8,256,256]{2,1,0:T(8,128)(2,1)S(1)} %get-tuple-element.30), channel_id=1, source_target_pairs={{0,1},{1,0},{2,3},{3,2},{4,5},{5,4},{6,7},{7,6},{8,9},{9,8},{10,11... | collective-permute-start | bytes 3145736 | tf_op jit(solution)/shard_map/ppermute | solution.py:255
  5.3 0.0 copy-done.1
  5.4 0.1 cosine_multiply_fusion.basis_ref
  5.5 0.0 copy-done
  5.5 0.6 shard_map.60
  6.1 0.5 shard_map.61.refs_0_
  6.6 1.4 %collective-permute-done.refs_1_ = bf16[8,256,256]{2,1,0:T(8,128)(2,1)S(1)} collective-permute-done((bf16[8,256,256]{2,1,0:T(8,128)(2,1)S(1)}, bf16[8,256,256]{2,1,0:T(8,128)(2,1)S(1)}, u32[]{:S(2)}, u32[]{:S(2)}) %collective-permute-start) | collective-permute-done | bytes 1048608 | tf_op jit(solution)/shard_map/ppermute | solution.py:255
  8.0 0.1 shard_map.62
  8.1 7.8 %collective-permute-start.3 = (bf16[4,256,256]{2,1,0:T(8,128)(2,1)S(1)}, bf16[4,256,256]{2,1,0:T(8,128)(2,1)S(1)}, u32[]{:S(2)}, u32[]{:S(2)}) collective-permute-start(bf16[4,256,256]{2,1,0:T(8,128)(2,1)S(1)} %shard_map.62), channel_id=1, source_target_pairs={{0,6},{1,3},{2,4},{3,1},{4,2},{5,7},{6,0},{7,5},{8,14},{9,11},{10,... | collective-permute-start | bytes 1572872 | tf_op jit(solution)/shard_map/ppermute | solution.py:255
  15.9 0.5 shard_map.63
  16.3 0.1 shard_map.64
  16.5 1.9 %collective-permute-start.2 = (bf16[4,256,256]{2,1,0:T(8,128)(2,1)S(1)}, bf16[4,256,256]{2,1,0:T(8,128)(2,1)S(1)}, u32[]{:S(2)}, u32[]{:S(2)}) collective-permute-start(bf16[4,256,256]{2,1,0:T(8,128)(2,1)S(1)} %shard_map.64), channel_id=1, source_target_pairs={{0,6},{1,3},{2,4},{3,1},{4,2},{5,7},{6,0},{7,5},{8,14},{9,11},{10,... | collective-permute-start | bytes 1572872 | tf_op jit(solution)/shard_map/ppermute | solution.py:255
  18.4 1.9 %collective-permute-start.1 = (bf16[8,256,256]{2,1,0:T(8,128)(2,1)S(1)}, bf16[8,256,256]{2,1,0:T(8,128)(2,1)S(1)}, u32[]{:S(2)}, u32[]{:S(2)}) collective-permute-start(bf16[8,256,256]{2,1,0:T(8,128)(2,1)S(1)} %shard_map.63), channel_id=1, source_target_pairs={{0,1},{1,0},{2,3},{3,2},{4,5},{5,4},{6,7},{7,6},{8,9},{9,8},{10,11... | collective-permute-start | bytes 3145736 | tf_op jit(solution)/shard_map/ppermute | solution.py:255
  20.3 0.5 shard_map.65.refs_0_
  20.8 2.2 %collective-permute-done.3.refs_2_ = bf16[4,256,256]{2,1,0:T(8,128)(2,1)S(1)} collective-permute-done((bf16[4,256,256]{2,1,0:T(8,128)(2,1)S(1)}, bf16[4,256,256]{2,1,0:T(8,128)(2,1)S(1)}, u32[]{:S(2)}, u32[]{:S(2)}) %collective-permute-start.3) | collective-permute-done | bytes 524320 | tf_op jit(solution)/shard_map/ppermute | solution.py:255
  23.0 0.0 collective-permute-done.1.refs_1_
  23.0 0.2 shard_map.67
  23.2 1.9 %collective-permute-start.4 = (bf16[1,256,256]{2,1,0:T(8,128)(2,1)S(1)}, bf16[1,256,256]{2,1,0:T(8,128)(2,1)S(1)}, u32[]{:S(2)}, u32[]{:S(2)}) collective-permute-start(bf16[1,256,256]{2,1,0:T(8,128)(2,1)S(1)} %get-tuple-element.36), channel_id=1, source_target_pairs={{0,2},{1,7},{2,0},{3,5},{4,6},{5,3},{6,4},{7,1},{8,10},{9,15},{10,... | collective-permute-start | bytes 393224 | tf_op jit(solution)/shard_map/ppermute | solution.py:255
  25.1 3.9 %collective-permute-start.7 = (bf16[1,256,256]{2,1,0:T(8,128)(2,1)S(1)}, bf16[1,256,256]{2,1,0:T(8,128)(2,1)S(1)}, u32[]{:S(2)}, u32[]{:S(2)}) collective-permute-start(bf16[1,256,256]{2,1,0:T(8,128)(2,1)S(1)} %get-tuple-element.43), channel_id=1, source_target_pairs={{0,2},{1,7},{2,0},{3,5},{4,6},{5,3},{6,4},{7,1},{8,10},{9,15},{10,... | collective-permute-start | bytes 393224 | tf_op jit(solution)/shard_map/ppermute | solution.py:255
  29.1 0.0 collective-permute-done.2.refs_2_
  29.1 0.2 shard_map.66
  29.3 0.8 %collective-permute-done.4.refs_1_ = bf16[1,256,256]{2,1,0:T(8,128)(2,1)S(1)} collective-permute-done((bf16[1,256,256]{2,1,0:T(8,128)(2,1)S(1)}, bf16[1,256,256]{2,1,0:T(8,128)(2,1)S(1)}, u32[]{:S(2)}, u32[]{:S(2)}) %collective-permute-start.4) | collective-permute-done | bytes 131104 | tf_op jit(solution)/shard_map/ppermute | solution.py:255
  30.1 6.5 %collective-permute-start.5 = (bf16[1,256,256]{2,1,0:T(8,128)(2,1)S(1)}, bf16[1,256,256]{2,1,0:T(8,128)(2,1)S(1)}, u32[]{:S(2)}, u32[]{:S(2)}) collective-permute-start(bf16[1,256,256]{2,1,0:T(8,128)(2,1)S(1)} %shard_map.68), channel_id=1, source_target_pairs={{0,8},{1,25},{2,10},{3,27},{4,12},{5,29},{6,14},{7,31},{8,0},{9,17... | collective-permute-start | bytes 393224 | tf_op jit(solution)/shard_map/ppermute | solution.py:255
  36.6 1.9 %collective-permute-start.6 = (bf16[2,256,256]{2,1,0:T(8,128)(2,1)S(1)}, bf16[2,256,256]{2,1,0:T(8,128)(2,1)S(1)}, u32[]{:S(2)}, u32[]{:S(2)}) collective-permute-start(bf16[2,256,256]{2,1,0:T(8,128)(2,1)S(1)} %get-tuple-element.37), channel_id=1, source_target_pairs={{0,2},{1,7},{2,0},{3,5},{4,6},{5,3},{6,4},{7,1},{8,10},{9,15},{10,... | collective-permute-start | bytes 786440 | tf_op jit(solution)/shard_map/ppermute | solution.py:255
  38.5 0.0 collective-permute-done.7.refs_1_
  38.6 3.3 %collective-permute-start.8 = (bf16[1,256,256]{2,1,0:T(8,128)(2,1)S(1)}, bf16[1,256,256]{2,1,0:T(8,128)(2,1)S(1)}, u32[]{:S(2)}, u32[]{:S(2)}) collective-permute-start(bf16[1,256,256]{2,1,0:T(8,128)(2,1)S(1)} %shard_map.71), channel_id=1, source_target_pairs={{0,8},{1,25},{2,10},{3,27},{4,12},{5,29},{6,14},{7,31},{8,0},{9,17... | collective-permute-start | bytes 393224 | tf_op jit(solution)/shard_map/ppermute | solution.py:255
  41.9 3.6 %collective-permute-done.5.refs_1_ = bf16[1,256,256]{2,1,0:T(8,128)(2,1)S(1)} collective-permute-done((bf16[1,256,256]{2,1,0:T(8,128)(2,1)S(1)}, bf16[1,256,256]{2,1,0:T(8,128)(2,1)S(1)}, u32[]{:S(2)}, u32[]{:S(2)}) %collective-permute-start.5) | collective-permute-done | bytes 131104 | tf_op jit(solution)/shard_map/ppermute | solution.py:255
  45.5 0.0 collective-permute-done.6.back_ref.refs_1_
  45.5 0.5 shard_map.70
  46.0 9.8 %collective-permute-start.10 = (f32[32,128]{1,0:T(8,128)S(1)}, f32[32,128]{1,0:T(8,128)S(1)}, u32[]{:S(2)}, u32[]{:S(2)}) collective-permute-start(f32[32,128]{1,0:T(8,128)S(1)} %get-tuple-element.45), channel_id=1, source_target_pairs={{0,24},{1,9},{2,26},{3,11},{4,28},{5,13},{6,30},{7,15},{8,16},{9,1... | collective-permute-start | bytes 49160 | tf_op jit(solution)/shard_map/ppermute | solution.py:255
  55.8 1.9 %collective-permute-start.9 = (bf16[1,256,256]{2,1,0:T(8,128)(2,1)S(1)}, bf16[1,256,256]{2,1,0:T(8,128)(2,1)S(1)}, u32[]{:S(2)}, u32[]{:S(2)}) collective-permute-start(bf16[1,256,256]{2,1,0:T(8,128)(2,1)S(1)} %shard_map.72), channel_id=1, source_target_pairs={{0,24},{1,9},{2,26},{3,11},{4,28},{5,13},{6,30},{7,15},{8,16},{9,1... | collective-permute-start | bytes 393224 | tf_op jit(solution)/shard_map/ppermute | solution.py:255
  57.7 0.0 collective-permute-done.8.r2_ref.back_ref
  57.7 0.6 collective-permute-done.10.other_ref
  58.3 1.2 %shard_map.74 = bf16[16,32,128]{2,1,0:T(8,128)(2,1)} custom-call(bf16[1,256,256]{2,1,0:T(8,128)(2,1)S(1)} %get-tuple-element.41.near_ref, bf16[1,256,256]{2,1,0:T(8,128)(2,1)S(1)} %collective-permute-done.8.r2_ref.back_ref, f32[32,128]{1,0:T(8,128)S(1)} %get-tuple-element.27.own_ref, f32[32,128]{1,0:T(8,128)S(1)} %collective-permute-done.10.other_ref, ...), custom_call_target="tpu_custom_call" | custom-call | flops 20000000000 | tf_op jit(solution)/shard_map/pallas_call | solution.py:234
  59.5 5.5 %all-to-all-start = ((bf16[16,32,128]{2,1,0:T(8,128)(2,1)}), bf16[16,32,128]{2,1,0:T(8,128)(2,1)S(1)}, u32[]{:S(2)}, u32[]{:S(2)}) async-start(bf16[16,32,128]{2,1,0:T(8,128)(2,1)} %shard_map.74), calls=%async_computation | async-start | bytes 262144 | tf_op jit(solution)/shard_map/all_to_all | solution.py:305
  65.0 4.4 %collective-permute-done.9.r1_ref = bf16[1,256,256]{2,1,0:T(8,128)(2,1)S(1)} collective-permute-done((bf16[1,256,256]{2,1,0:T(8,128)(2,1)S(1)}, bf16[1,256,256]{2,1,0:T(8,128)(2,1)S(1)}, u32[]{:S(2)}, u32[]{:S(2)}) %collective-permute-start.9) | collective-permute-done | bytes 131104 | tf_op jit(solution)/shard_map/ppermute | solution.py:255
  69.3 1.9 %shard_map.73 = f32[1,256,256]{2,1,0:T(8,128)} custom-call(f32[1,256,256]{2,1,0:T(8,128)S(1)} %copy-done, bf16[1,256,256]{2,1,0:T(8,128)(2,1)S(1)} %get-tuple-element.41.near_ref, bf16[1,256,256]{2,1,0:T(8,128)(2,1)S(1)} %collective-permute-done.8.r2_ref.back_ref, bf16[1,256,256]{2,1,0:T(8,128)(2,1)S(1)} %collective-permute-done.9.r1_ref, ...), custom_call_target="tpu_custom_call" | custom-call | flops 20000000000 | tf_op jit(solution)/shard_map/pallas_call | solution.py:234
  71.3 2.7 %all-to-all-done.every_ref = bf16[16,32,128]{2,1,0:T(8,128)(2,1)S(1)} async-done(((bf16[16,32,128]{2,1,0:T(8,128)(2,1)}), bf16[16,32,128]{2,1,0:T(8,128)(2,1)S(1)}, u32[]{:S(2)}, u32[]{:S(2)}) %all-to-all-start) | async-done | bytes 131104 | tf_op jit(solution)/shard_map/all_to_all | solution.py:305
  74.0 1.2 %shard_map.75 = f32[256,256]{1,0:T(8,128)} custom-call(bf16[16,32,128]{2,1,0:T(8,128)(2,1)S(1)} %all-to-all-done.every_ref, bf16[192,256]{1,0:T(8,128)(2,1)S(1)} %get-tuple-element.48.right_ref, bf16[256,192]{1,0:T(8,128)(2,1)S(1)} %get-tuple-element.49.left_ref), custom_call_target="tpu_custom_call" | custom-call | tf_op jit(solution)/shard_map/pallas_call | solution.py:234
  (7 shorter events, 0.2 us)
Async XLA Ops:
  0.6 4.7 %copy-start.1 = (s32[16]{0:T(128)S(1)}, s32[16]{0:T(128)}, u32[]{:S(2)}) copy-start(s32[16]{0:T(128)} %param.7) | copy-start | bytes 196
  0.6 4.9 %copy-start = (f32[1,256,256]{2,1,0:T(8,128)S(1)}, f32[1,256,256]{2,1,0:T(8,128)}, u32[]{:S(2)}) copy-start(f32[1,256,256]{2,1,0:T(8,128)} %momentum_ref.3) | copy-start | bytes 786436
  3.4 4.6 %collective-permute-start = (bf16[8,256,256]{2,1,0:T(8,128)(2,1)S(1)}, bf16[8,256,256]{2,1,0:T(8,128)(2,1)S(1)}, u32[]{:S(2)}, u32[]{:S(2)}) collective-permute-start(bf16[8,256,256]{2,1,0:T(8,128)(2,1)S(1)} %get-tuple-element.30), channel_id=1, source_target_pairs={{0,1},{1,0},{2,3},{3,2},{4,5},{5,4},{6,7},{7,6},{8,9},{9,8},{10,11... | collective-permute-start | bytes 3145736 | tf_op jit(solution)/shard_map/ppermute | solution.py:255
  8.1 14.9 %collective-permute-start.3 = (bf16[4,256,256]{2,1,0:T(8,128)(2,1)S(1)}, bf16[4,256,256]{2,1,0:T(8,128)(2,1)S(1)}, u32[]{:S(2)}, u32[]{:S(2)}) collective-permute-start(bf16[4,256,256]{2,1,0:T(8,128)(2,1)S(1)} %shard_map.62), channel_id=1, source_target_pairs={{0,6},{1,3},{2,4},{3,1},{4,2},{5,7},{6,0},{7,5},{8,14},{9,11},{10,... | collective-permute-start | bytes 1572872 | tf_op jit(solution)/shard_map/ppermute | solution.py:255
  16.5 12.6 %collective-permute-start.2 = (bf16[4,256,256]{2,1,0:T(8,128)(2,1)S(1)}, bf16[4,256,256]{2,1,0:T(8,128)(2,1)S(1)}, u32[]{:S(2)}, u32[]{:S(2)}) collective-permute-start(bf16[4,256,256]{2,1,0:T(8,128)(2,1)S(1)} %shard_map.64), channel_id=1, source_target_pairs={{0,6},{1,3},{2,4},{3,1},{4,2},{5,7},{6,0},{7,5},{8,14},{9,11},{10,... | collective-permute-start | bytes 1572872 | tf_op jit(solution)/shard_map/ppermute | solution.py:255
  18.4 4.6 %collective-permute-start.1 = (bf16[8,256,256]{2,1,0:T(8,128)(2,1)S(1)}, bf16[8,256,256]{2,1,0:T(8,128)(2,1)S(1)}, u32[]{:S(2)}, u32[]{:S(2)}) collective-permute-start(bf16[8,256,256]{2,1,0:T(8,128)(2,1)S(1)} %shard_map.63), channel_id=1, source_target_pairs={{0,1},{1,0},{2,3},{3,2},{4,5},{5,4},{6,7},{7,6},{8,9},{9,8},{10,11... | collective-permute-start | bytes 3145736 | tf_op jit(solution)/shard_map/ppermute | solution.py:255
  23.2 6.9 %collective-permute-start.4 = (bf16[1,256,256]{2,1,0:T(8,128)(2,1)S(1)}, bf16[1,256,256]{2,1,0:T(8,128)(2,1)S(1)}, u32[]{:S(2)}, u32[]{:S(2)}) collective-permute-start(bf16[1,256,256]{2,1,0:T(8,128)(2,1)S(1)} %get-tuple-element.36), channel_id=1, source_target_pairs={{0,2},{1,7},{2,0},{3,5},{4,6},{5,3},{6,4},{7,1},{8,10},{9,15},{10,... | collective-permute-start | bytes 393224 | tf_op jit(solution)/shard_map/ppermute | solution.py:255
  25.1 13.4 %collective-permute-start.7 = (bf16[1,256,256]{2,1,0:T(8,128)(2,1)S(1)}, bf16[1,256,256]{2,1,0:T(8,128)(2,1)S(1)}, u32[]{:S(2)}, u32[]{:S(2)}) collective-permute-start(bf16[1,256,256]{2,1,0:T(8,128)(2,1)S(1)} %get-tuple-element.43), channel_id=1, source_target_pairs={{0,2},{1,7},{2,0},{3,5},{4,6},{5,3},{6,4},{7,1},{8,10},{9,15},{10,... | collective-permute-start | bytes 393224 | tf_op jit(solution)/shard_map/ppermute | solution.py:255
  30.1 15.3 %collective-permute-start.5 = (bf16[1,256,256]{2,1,0:T(8,128)(2,1)S(1)}, bf16[1,256,256]{2,1,0:T(8,128)(2,1)S(1)}, u32[]{:S(2)}, u32[]{:S(2)}) collective-permute-start(bf16[1,256,256]{2,1,0:T(8,128)(2,1)S(1)} %shard_map.68), channel_id=1, source_target_pairs={{0,8},{1,25},{2,10},{3,27},{4,12},{5,29},{6,14},{7,31},{8,0},{9,17... | collective-permute-start | bytes 393224 | tf_op jit(solution)/shard_map/ppermute | solution.py:255
  36.6 8.9 %collective-permute-start.6 = (bf16[2,256,256]{2,1,0:T(8,128)(2,1)S(1)}, bf16[2,256,256]{2,1,0:T(8,128)(2,1)S(1)}, u32[]{:S(2)}, u32[]{:S(2)}) collective-permute-start(bf16[2,256,256]{2,1,0:T(8,128)(2,1)S(1)} %get-tuple-element.37), channel_id=1, source_target_pairs={{0,2},{1,7},{2,0},{3,5},{4,6},{5,3},{6,4},{7,1},{8,10},{9,15},{10,... | collective-permute-start | bytes 786440 | tf_op jit(solution)/shard_map/ppermute | solution.py:255
  38.6 19.2 %collective-permute-start.8 = (bf16[1,256,256]{2,1,0:T(8,128)(2,1)S(1)}, bf16[1,256,256]{2,1,0:T(8,128)(2,1)S(1)}, u32[]{:S(2)}, u32[]{:S(2)}) collective-permute-start(bf16[1,256,256]{2,1,0:T(8,128)(2,1)S(1)} %shard_map.71), channel_id=1, source_target_pairs={{0,8},{1,25},{2,10},{3,27},{4,12},{5,29},{6,14},{7,31},{8,0},{9,17... | collective-permute-start | bytes 393224 | tf_op jit(solution)/shard_map/ppermute | solution.py:255
  46.0 12.3 %collective-permute-start.10 = (f32[32,128]{1,0:T(8,128)S(1)}, f32[32,128]{1,0:T(8,128)S(1)}, u32[]{:S(2)}, u32[]{:S(2)}) collective-permute-start(f32[32,128]{1,0:T(8,128)S(1)} %get-tuple-element.45), channel_id=1, source_target_pairs={{0,24},{1,9},{2,26},{3,11},{4,28},{5,13},{6,30},{7,15},{8,16},{9,1... | collective-permute-start | bytes 49160 | tf_op jit(solution)/shard_map/ppermute | solution.py:255
  55.8 13.6 %collective-permute-start.9 = (bf16[1,256,256]{2,1,0:T(8,128)(2,1)S(1)}, bf16[1,256,256]{2,1,0:T(8,128)(2,1)S(1)}, u32[]{:S(2)}, u32[]{:S(2)}) collective-permute-start(bf16[1,256,256]{2,1,0:T(8,128)(2,1)S(1)} %shard_map.72), channel_id=1, source_target_pairs={{0,24},{1,9},{2,26},{3,11},{4,28},{5,13},{6,30},{7,15},{8,16},{9,1... | collective-permute-start | bytes 393224 | tf_op jit(solution)/shard_map/ppermute | solution.py:255
  59.5 14.5 %all-to-all-start = ((bf16[16,32,128]{2,1,0:T(8,128)(2,1)}), bf16[16,32,128]{2,1,0:T(8,128)(2,1)S(1)}, u32[]{:S(2)}, u32[]{:S(2)}) async-start(bf16[16,32,128]{2,1,0:T(8,128)(2,1)} %shard_map.74), calls=%async_computation | async-start | bytes 262144 | tf_op jit(solution)/shard_map/all_to_all | solution.py:305
